TPU v7x, 256 devices: a whole 4x4x8 slice. The times are simulated.
256 devices in a mesh: stator: 64 (over z, y, core), axial: 4 (over x).
Axes of the slice: x: 4, y: 4, z: 8, core: 2. Of those that a mesh axis runs over, the one named last changes fastest.
Arguments:
- coeffs: float32 [32, 262144], P(None, ('stator', 'axial')), may hold values from -6 to 6
- elem_edge: int32 [6, 262144], P(None, ('stator', 'axial')), may hold values from 0 to 1151
- curl_map: float32 [3, 6, 262144], P(None, None, ('stator', 'axial')), may hold values from -1.8 to 1.8
- jacobian: bfloat16 [6, 32, 262144], P(None, None, ('stator', 'axial')), may hold values from -4 to 10, as said below
- flux_fwd: bfloat16 [3, 32, 262144], P(None, None, ('stator', 'axial')), may hold values from -6 to 6
- density: float32 [262144], P(('stator', 'axial')), may hold values from 0.05 to 1
- mortar: float32 [128, 128], replicated, may hold values from -0.5 to 0.5
- gap_peer: int32 [32768, 1], P(('stator', 'axial')), may hold values from 0 to 63; in each aligned block of 128 rows (0 to 127, 128 to 255, ...) at most 4 rows name the same one
- gap_block: int32 [32768], P(('stator', 'axial')), may hold values from 0 to 1
Outputs:
- adjoint: float32 [32, 262144], P(None, ('stator', 'axial'))
- density_grad: float32 [262144], P(('stator', 'axial'))
Inputs may be any that keep to these rules, and one draw needn't show every extreme that they name: `elem_edge`: each entry indexes the device's own 1024 edges followed by the first 128 edges of the next axial slab. `gap_peer`: row s * 4 + b of one device names the stator index whose face meets rotor face block b at sample s; at most 4 rows of one device name the same index, and exactly 4 for some index. `jacobian`: each sample's six components form a symmetric matrix with positive diagonal; each off-diagonal entry is at most 0.41 times the square root of the product of its two diagonal entries, so the matrix is positive definite.
All inputs are finite; a program needn't handle non-finite values.
Results may differ from a plain program's by a relative error of at most 0.0003.
Values sent between devices are 32-bit elements; how exact they have to be, the bound alone decides.
A program may use at most 64 MiB of HBM per device.

v0:
```python
import math

import jax
import jax.numpy as jnp
from jax import lax
from jax.sharding import PartitionSpec as P

S = 32
GE = 128
GB = 4
QB = 2


PENALTY = 4.0
SIMP_POWER = 3.0


def shifted(value, axis, steps):
    count = lax.axis_size(axis)
    leading, last = (max(0, -steps), min(count, count - steps))
    return lax.ppermute(value, axis, [(source, source + steps) for source in range(leading, last)])


def dft_table(count):
    rows = jnp.arange(count, dtype=jnp.float32)[:, None]
    index = jnp.arange(count, dtype=jnp.int32)
    harmonic = ((index + 1) // 2).astype(jnp.float32)[None, :]
    is_sine = ((index % 2 == 0) & (index > 0))[None, :]
    angle = 2.0 * math.pi * harmonic * rows / count
    table = jnp.where(is_sine, jnp.sin(angle), jnp.cos(angle))
    return table * jnp.float32(math.sqrt(2.0 / count))


def element_work(extended, elem_edge, curl_map, jacobian, flux_fwd, density):
    samples = extended.shape[0]
    values = extended[:, elem_edge]
    flux_lam = jnp.einsum("cke,ske->cse", curl_map, values, precision=lax.Precision.HIGHEST)
    jac = jacobian.astype(jnp.float32)
    field_h = jnp.stack(
        [
            jac[0] * flux_lam[0] + jac[3] * flux_lam[1] + jac[4] * flux_lam[2],
            jac[3] * flux_lam[0] + jac[1] * flux_lam[1] + jac[5] * flux_lam[2],
            jac[4] * flux_lam[0] + jac[5] * flux_lam[1] + jac[2] * flux_lam[2],
        ]
    )
    element_terms = jnp.einsum("cke,cse->kes", curl_map, field_h, precision=lax.Precision.HIGHEST)
    summed = jax.ops.segment_sum(
        element_terms.reshape(-1, samples), elem_edge.reshape(-1), num_segments=extended.shape[1]
    )
    energy = jnp.sum(flux_lam * flux_fwd.astype(jnp.float32), axis=(0, 1))
    grad = SIMP_POWER * density * density * energy / samples
    return (summed.T, grad)


def on_device(
    coeffs, elem_edge, curl_map, jacobian, flux_fwd, density, mortar, gap_peer, gap_block
):
    stators = lax.axis_size("stator")
    edge_count = coeffs.shape[1]
    face_count = edge_count // 8
    table = dft_table(S)
    in_time = jnp.dot(table, coeffs, precision=lax.Precision.HIGHEST)
    upper_rim = shifted(in_time[:, :face_count], "axial", -1)
    extended = jnp.concatenate([in_time, upper_rim], 1)
    res_ext, density_grad = element_work(extended, elem_edge, curl_map, jacobian, flux_fwd, density)
    lower_rim = shifted(res_ext[:, edge_count:], "axial", 1)
    residual = res_ext[:, :edge_count]
    residual = residual.at[:, :face_count].add(lower_rim)
    rotor_start = edge_count - GB * GE
    rotor_rows = in_time[:, rotor_start:].reshape(S * GB, GE)
    stator_rows = in_time[:, face_count : face_count + QB * GE].reshape(S * QB, GE)
    mapped = jnp.dot(stator_rows, mortar, precision=lax.Precision.HIGHEST)
    owners = gap_peer[:, 0]
    target = (jnp.arange(S, dtype=jnp.int32)[:, None] * QB + gap_block.reshape(S, GB)).reshape(-1)
    everyone = lax.all_gather(mapped, "stator", axis=0, tiled=True)
    lookup = owners * (S * QB) + target
    jump_rows = rotor_rows - everyone[lookup]
    rotor_term = PENALTY * jump_rows
    jump_sums = jax.ops.segment_sum(jump_rows, lookup, num_segments=stators * S * QB)
    own_jumps = lax.psum_scatter(jump_sums, "stator", scatter_dimension=0, tiled=True)
    stator_term = -PENALTY * jnp.dot(own_jumps, mortar.T, precision=lax.Precision.HIGHEST)
    residual = residual.at[:, rotor_start:].add(rotor_term.reshape(S, GB * GE))
    residual = residual.at[:, face_count : face_count + QB * GE].add(
        stator_term.reshape(S, QB * GE)
    )
    adjoint = jnp.dot(table.T, residual, precision=lax.Precision.HIGHEST)
    return (adjoint, density_grad)


def solution(mesh):
    placed = (
        P(None, ("stator", "axial")),
        P(None, ("stator", "axial")),
        P(None, None, ("stator", "axial")),
        P(None, None, ("stator", "axial")),
        P(None, None, ("stator", "axial")),
        P(("stator", "axial")),
        P(),
        P(("stator", "axial"), None),
        P(("stator", "axial")),
    )
    return jax.shard_map(
        on_device,
        mesh=mesh,
        in_specs=placed,
        out_specs=(P(None, ("stator", "axial")), P(("stator", "axial"))),
        check_vma=False,
    )
```

profile of v0, /device:TPU:1, one launch (start us, length us, event | category | flops | bytes accessed | tf_op | source)
XLA Modules:
  0.0 261.4 jit_solution(4632753568492245992)
XLA Ops:
  7.2 0.0 copy-start
  7.2 0.0 copy-start.4
  7.2 0.0 all-gather.2.cloned.1.call-start
  7.3 0.8 copy-done
  8.1 0.3 fusion.17
  8.4 1.6 fusion.33
  10.1 0.0 all-gather.2.cloned.1.call-update
  10.1 0.0 reduce-scatter.2.cloned.1.call-start
  10.2 1.3 collective-permute-start
  11.5 0.1 add.115
  11.6 0.1 add.116
  11.7 0.8 compare_select_fusion
  12.5 0.7 compare_select_fusion.1
  13.1 1.4 reshape.157
  14.5 2.0 convert_element_type.16
  16.5 0.0 copy-done.4
  16.5 0.9 copy.57
  17.3 0.0 collective-permute-done
  17.4 0.2 copy.55
  17.6 20.9 %gather_fusion = f32[6144,32]{1,0:T(8,128)} fusion(f32[32,1152]{0,1:T(8,128)S(1)} %copy.55, s32[6144]{0:T(1024)S(1)} %broadcast_clamp_fusion), kind=kCustom, calls=%fused_computation | custom fusion | bytes 1597440 | tf_op jit(solution)/shard_map/gather | solution.py:36
  38.5 11.4 %fusion = f32[1024,32,3]{1,2,0:T(4,128)} fusion(f32[3,6,1024]{1,0,2:T(4,128)S(1)} %copy.57, f32[6,1024,32]{2,1,0:T(8,128)} %bitcast.22), kind=kOutput, calls=%fused_computation.4 | convolution fusion | flops 7077888 | bytes 1253376 | tf_op jit(solution)/shard_map/cke,ske->cse/dot_general | solution.py:37
  49.9 1.8 copy.58
  51.8 0.0 copy-done.1
  51.8 0.1 fusion.11
  51.9 1.8 copy.59
  53.7 10.0 %convolution_bitcast_fusion = f32[6,1024,32]{2,0,1:T(8,128)S(1)} fusion(f32[3,32,1024]{1,0,2:T(4,128)} %copy.59, f32[3,6,1024]{1,0,2:T(4,128)S(1)} %copy.57), kind=kOutput, calls=%fused_computation.7 | convolution fusion | flops 7077888 | bytes 1253376 | tf_op jit(solution)/shard_map/cke,cse->kes/dot_general | solution.py:46
  63.7 2.2 copy.64
  65.9 33.8 %scatter_custom_fusion = f32[1152,32]{1,0:T(8,128)S(1)} fusion(s32[6144]{0:T(1024)} %reshape.157, f32[6144,32]{1,0:T(8,128)} %bitcast.24, f32[]{:T(128)} %constant.130.clone.1), kind=kCustom, calls=%fused_computation.13 | custom fusion | flops 196608 | bytes 147968 | tf_op jit(solution)/shard_map/scatter-add | solution.py:47
  99.8 0.2 copy.63
  100.0 4.6 %collective-permute-start.1 = (f32[32,128]{1,0:T(8,128)S(1)}, f32[32,128]{1,0:T(8,128)S(1)}, u32[]{:S(2)}, u32[]{:S(2)}) collective-permute-start(f32[32,128]{1,0:T(8,128)S(1)} %slice.142), channel_id=1, source_target_pairs={{0,1},{1,2},{2,3},{4,5},{5,6},{6,7},{8,9},{9,10},{10,11},{12,13},{... | collective-permute-start | bytes 49160 | tf_op jit(solution)/shard_map/ppermute | solution.py:21
  104.6 0.6 compare_reduce_fusion.1
  105.2 0.2 collective-permute-done.1
  105.4 0.6 fusion.15
  106.0 0.0 all-gather.2.cloned.1.call-done
  106.1 2.2 gather_fusion.1
  108.4 0.0 copy-start.3
  108.4 0.0 copy-start.5
  108.4 0.0 copy-start.2
  108.4 2.5 scatter_custom_fusion.1
  110.9 0.0 reduce-scatter.2.cloned.1.call-update
  110.9 0.6 compare_reduce_fusion
  111.5 0.0 copy-done.3
  111.5 0.1 multiply_reduce_fusion
  111.6 0.6 fusion.27
  112.2 139.6 %reduce-scatter.2.cloned.1.call-done = f32[64,128]{1,0:T(8,128)} async-done(((f32[4096,128]{1,0:T(8,128)}), f32[64,128]{1,0:T(8,128)}) %reduce-scatter.2.cloned.1.call-update) | async-done | bytes 32784 | tf_op jit(solution)/shard_map/reduce_scatter | solution.py:80
  251.8 1.0 convolution_multiply_fusion
  252.8 0.7 fusion.14
  253.5 1.1 fusion.16
  (20 shorter events, 0.2 us)
Async XLA Ops:
  7.2 0.9 copy-start
  7.2 9.3 %copy-start.4 = (f32[3,6,1024]{2,1,0:T(8,128)S(1)}, f32[3,6,1024]{2,1,0:T(8,128)}, u32[]{:S(2)}) copy-start(f32[3,6,1024]{2,1,0:T(8,128)} %param.17) | copy-start | bytes 221188
  7.2 98.9 %all-gather.2.cloned.1.call-start = ((), (), s32[]{:S(2)}) async-start(), calls=%async_computation.1 | async-start | bytes 2129920 | tf_op jit(solution)/shard_map/all_gather | solution.py:75
  10.1 241.7 %reduce-scatter.2.cloned.1.call-start = ((), (), s32[]{:S(2)}) async-start(), calls=%async_computation.2 | async-start | bytes 2129920 | tf_op jit(solution)/shard_map/reduce_scatter | solution.py:80
  10.2 7.2 %collective-permute-start = (f32[32,128]{1,0:T(8,128)S(1)}, f32[32,128]{1,0:T(8,128)S(1)}, u32[]{:S(2)}, u32[]{:S(2)}) collective-permute-start(f32[32,128]{1,0:T(8,128)S(1)} %slice.131), channel_id=1, source_target_pairs={{1,0},{2,1},{3,2},{5,4},{6,5},{7,6},{9,8},{10,9},{11,10},{13,12},{... | collective-permute-start | bytes 49160 | tf_op jit(solution)/shard_map/ppermute | solution.py:21
  49.9 1.9 copy-start.1
  100.0 5.4 %collective-permute-start.1 = (f32[32,128]{1,0:T(8,128)S(1)}, f32[32,128]{1,0:T(8,128)S(1)}, u32[]{:S(2)}, u32[]{:S(2)}) collective-permute-start(f32[32,128]{1,0:T(8,128)S(1)} %slice.142), channel_id=1, source_target_pairs={{0,1},{1,2},{2,3},{4,5},{5,6},{6,7},{8,9},{9,10},{10,11},{12,13},{... | collective-permute-start | bytes 49160 | tf_op jit(solution)/shard_map/ppermute | solution.py:21
  108.4 3.2 %copy-start.3 = (bf16[3,32,1024]{2,1,0:T(8,128)(2,1)S(1)}, bf16[3,32,1024]{2,1,0:T(8,128)(2,1)}, u32[]{:S(2)}) copy-start(bf16[3,32,1024]{2,1,0:T(8,128)(2,1)} %param.19) | copy-start | bytes 589828
  108.4 3.2 %copy-start.5 = (f32[1024]{0:T(1024)S(1)}, f32[1024]{0:T(1024)}, u32[]{:S(2)}) copy-start(f32[1024]{0:T(1024)} %param.20) | copy-start | bytes 12292
  108.4 143.4 %copy-start.2 = (f32[128,128]{1,0:T(8,128)S(1)}, f32[128,128]{1,0:T(8,128)}, u32[]{:S(2)}) copy-start(f32[128,128]{1,0:T(8,128)} %param.21) | copy-start | bytes 196612
Sparse Core Ops, SparseCore 0:
  11.4 81.5 all-gather.1
  111.0 140.7 reduce-scatter.1
where the time goes:
time: 266 us; the launch traced here: 261 us
  waiting for transfers between devices  140 us (53%)
  other arithmetic  43.1 us (16%)
  local copies, waits for them, and re-layouts  32.7 us (12%)
  matrix products  25.5 us (10%)
  between operations  14.3 us (5%)
  starting transfers between devices  5.95 us (2%)
    reduce_scatter x1, waiting for transfers between devices, on_device(): lax.psum_scatter(jump_sums, 'stator', scatter_dimension=0, tiled=True)  140 us
    scatter-add x1, other arithmetic, element_work(): jax.ops.segment_sum(element_terms.reshape(-1, samples), elem_edge.reshape...  33.8 us
    gather x1, local copies, waits for them, and re-layouts, element_work(): values = extended[:, elem_edge]  20.9 us
    dot_general x1, matrix products, element_work(): jnp.einsum('cke,ske->cse', curl_map, values, precision=lax.Precision.HIGH...  11.4 us
    dot_general x1, matrix products, element_work(): jnp.einsum('cke,cse->kes', curl_map, field_h, precision=lax.Precision.HIG...  10 us
    ppermute x2, starting transfers between devices, shifted(): lax.ppermute(value, axis, [(source, source + steps) for source in range(l...  5.87 us
  transfers between devices with their start and end apart: 4, of which 2 were waited for; matrix products, arithmetic and copies ran while one was open for 35% of the time, Pallas kernels for 0%

commit v1 on v0

v1 whole, which is shorter than its diff:
```python
import functools
import math

import jax
import jax.numpy as jnp
import numpy as np
from jax import lax
from jax.experimental import pallas as pl
from jax.experimental.pallas import tpu as pltpu
from jax.sharding import PartitionSpec as P

GE = 128
GB = 4
QB = 2
CAP = 4
PENALTY = 4.0
SIMP_POWER = 3.0
CHUNK = 256

MESH = pl.DeviceIdType.MESH
F32 = jnp.float32
BF16 = jnp.bfloat16
NN = (((1,), (0,)), ((), ()))
NT = (((1,), (1,)), ((), ()))


def dft_table(count):
    rows = np.arange(count, dtype=np.float64)[:, None]
    index = np.arange(count)
    harmonic = ((index + 1) // 2).astype(np.float64)[None, :]
    is_sine = ((index % 2 == 0) & (index > 0))[None, :]
    angle = 2.0 * math.pi * harmonic * rows / count
    table = np.where(is_sine, np.sin(angle), np.cos(angle))
    return (table * math.sqrt(2.0 / count)).astype(np.float32)


def triple(table):
    high = table.astype(jnp.bfloat16)
    low = (table - high.astype(np.float32)).astype(jnp.bfloat16)
    return np.concatenate([high, high, low], 1)


def split(value):
    high = value.astype(BF16)
    return high, (value - high.astype(F32)).astype(BF16)


def mul(a, b, dims=NN):
    return lax.dot_general(a, b, dims, preferred_element_type=F32)


def table_dot(table, value):
    high, low = split(value)
    return mul(table, jnp.concatenate([high, low, high], 0))


def dot3(a, b, dims=NN):
    a_high, a_low = split(a)
    b_high, b_low = split(b)
    return mul(a_high, b_high, dims) + mul(a_high, b_low, dims) + mul(a_low, b_high, dims)


def side_by_side(value):
    return jnp.concatenate(split(value), 1)


def add_halves(value):
    half = value.shape[1] // 2
    return value[:, :half] + value[:, half:]


def as_bf16(mask):
    return jnp.where(mask, F32(1), F32(0)).astype(BF16)


def iota(shape, dim):
    return lax.broadcasted_iota(jnp.int32, shape, dim)


def kernel(
    stators,
    axials,
    coeffs,
    edge,
    curl,
    jac,
    fwd,
    density,
    mortar,
    packed,
    table,
    table_t,
    adjoint,
    grad,
    upper,
    lower_out,
    lower_in,
    meta,
    sendbuf,
    recvbuf,
    mapped_rows,
    in_time,
    ext,
    hot,
    acc,
    upper_send,
    upper_recv,
    lower_send,
    lower_recv,
    meta_send,
    meta_recv,
    data_send,
    data_recv,
):
    samples, edges = coeffs.shape
    face = edges // 8
    extended = edges + face
    rows = samples * GB
    slots = 2 * CAP
    rotor_start = edges - GB * GE
    me, ax = lax.axis_index("stator"), lax.axis_index("axial")
    above, below = lax.rem(ax + 1, axials), lax.rem(ax + axials - 1, axials)

    barrier = pltpu.get_barrier_semaphore()

    def greet(step, carry):
        peer = lax.rem(me + step, stators)
        pl.semaphore_signal(barrier, inc=1, device_id=(peer, ax), device_id_type=MESH)
        return carry

    for other in (above, below):
        pl.semaphore_signal(barrier, inc=1, device_id=(me, other), device_id_type=MESH)
    lax.fori_loop(1, stators, greet, 0)

    a, b = iota((rows, rows), 0), iota((rows, rows), 1)
    own_order = b == lax.rem(a, samples) * GB + lax.div(a, samples)
    listed = packed[...].astype(F32)
    col = jnp.sum(jnp.where(own_order, listed, 0.0), axis=1, keepdims=True)
    row = jnp.sum(jnp.where(a == b, col, 0.0), axis=0, keepdims=True)
    peer_col, peer_row = jnp.floor(col * 0.5), jnp.floor(row * 0.5)
    same = peer_col == peer_row
    rank_row = jnp.sum(jnp.where(same & (a < b), 1.0, 0.0), axis=0, keepdims=True)
    rank_col = jnp.sum(jnp.where(same & (b < a), 1.0, 0.0), axis=1, keepdims=True)
    slot_row = (peer_row * slots + rank_row).astype(jnp.int32)
    slot_col = (peer_col * slots + rank_col).astype(jnp.int32)
    code_row = (peer_row * CAP + rank_row) * QB + (row - 2.0 * peer_row)
    own_slots = pl.ds(pl.multiple_of(me * slots, slots), slots)
    meta[own_slots, :] = jnp.broadcast_to(code_row, (slots, rows))

    pl.semaphore_wait(barrier, stators - 1 + 2)

    upper_copy = pltpu.make_async_remote_copy(
        src_ref=coeffs.at[:, pl.ds(0, face)],
        dst_ref=upper,
        send_sem=upper_send,
        recv_sem=upper_recv,
        device_id=(me, below),
        device_id_type=MESH,
    )
    upper_copy.start()

    def send_meta(step, carry):
        peer = lax.rem(me + step, stators)
        pltpu.make_async_remote_copy(
            src_ref=meta.at[own_slots, :],
            dst_ref=meta.at[own_slots, :],
            send_sem=meta_send,
            recv_sem=meta_recv,
            device_id=(peer, ax),
            device_id_type=MESH,
        ).start()
        return carry

    lax.fori_loop(1, stators, send_meta, 0)

    in_time[...] = table_dot(table[...], coeffs[...])
    own_high, own_low = split(in_time[...])
    ext[0:samples, 0:edges] = own_high
    ext[samples : 2 * samples, 0:edges] = own_low
    for q in range(QB):
        here = in_time[:, face + q * GE : face + (q + 1) * GE]
        mapped_rows[q * samples : (q + 1) * samples, :] = dot3(here, mortar[...])

    upper_copy.wait()
    inside = jnp.where(ax < axials - 1, F32(1), F32(0))
    rim_high, rim_low = split(table_dot(table[...], upper[...] * inside))
    ext[0:samples, edges:extended] = rim_high
    ext[samples : 2 * samples, edges:extended] = rim_low

    acc[...] = jnp.zeros_like(acc)

    def element_chunk(chunk, carry):
        lanes = pl.ds(pl.multiple_of(chunk * CHUNK, CHUNK), CHUNK)
        sub = iota((extended, CHUNK), 0).astype(jnp.int16)
        named = edge[:, lanes].astype(jnp.int16)
        for m in range(6):
            mask = sub == named[m : m + 1, :]
            hot[:, m * CHUNK : (m + 1) * CHUNK] = jnp.where(mask, BF16(1), BF16(0))
        values = mul(ext[...], hot[...])
        values = values[:samples] + values[samples:]
        maps = curl[:, :, lanes]
        flux = []
        for c in range(3):
            total = None
            for m in range(6):
                term = maps[c, m : m + 1, :] * values[:, m * CHUNK : (m + 1) * CHUNK]
                total = term if total is None else total + term
            flux.append(total)
        j = [jac[k, :, lanes].astype(F32) for k in range(6)]
        field = [
            j[0] * flux[0] + j[3] * flux[1] + j[4] * flux[2],
            j[3] * flux[0] + j[1] * flux[1] + j[5] * flux[2],
            j[4] * flux[0] + j[5] * flux[1] + j[2] * flux[2],
        ]
        energy = sum(flux[c] * fwd[c, :, lanes].astype(F32) for c in range(3))
        energy = jnp.sum(energy, axis=0, keepdims=True)
        dens = density[:, lanes]
        grad[:, lanes] = SIMP_POWER * dens * dens * energy / samples
        highs, lows = [], []
        for m in range(6):
            high, low = split(sum(maps[c, m : m + 1, :] * field[c] for c in range(3)))
            highs.append(high)
            lows.append(low)
        terms = jnp.concatenate([jnp.concatenate(highs, 1), jnp.concatenate(lows, 1)], 0)
        acc[...] += mul(terms, hot[...], NT)
        return carry

    chunks = edges // CHUNK
    lax.fori_loop(0, chunks // 2, element_chunk, 0)

    def all_meta(buf):
        return pltpu.make_async_copy(
            buf.at[pl.ds(0, (stators - 1) * slots), :],
            buf.at[pl.ds(0, (stators - 1) * slots), :],
            meta_recv,
        )

    all_meta(meta).wait()
    every = stators * slots
    place = iota((every, rows), 0)
    rank_here = lax.rem(place, CAP)
    wanted = lax.rem(place, slots) >= CAP
    codes = meta[...]
    mapped = mapped_rows[...]
    hits = [as_bf16(codes == ((me * CAP + rank_here) * QB + q).astype(F32)) for q in range(QB)]
    tiled = [jnp.concatenate([mapped[q * samples : (q + 1) * samples]] * GB, 0) for q in range(QB)]
    facing_rows = add_halves(
        mul(jnp.concatenate(hits, 1), side_by_side(jnp.concatenate(tiled, 0)))
    )
    rotor = jnp.concatenate(
        [in_time[:, rotor_start + b * GE : rotor_start + (b + 1) * GE] for b in range(GB)], 0
    )
    rotor_rows = add_halves(mul(as_bf16(place == slot_row), side_by_side(rotor)))
    sendbuf[...] = rotor_rows + jnp.where(wanted, facing_rows, 0.0)

    def send_data(step, carry):
        peer = lax.rem(me + step, stators)
        pltpu.make_async_remote_copy(
            src_ref=sendbuf.at[pl.ds(pl.multiple_of(peer * slots, slots), slots), :],
            dst_ref=recvbuf.at[own_slots, :],
            send_sem=data_send,
            recv_sem=data_recv,
            device_id=(peer, ax),
            device_id_type=MESH,
        ).start()
        return carry

    lax.fori_loop(1, stators, send_data, 0)
    recvbuf[own_slots, :] = sendbuf[own_slots, :]

    place_t = iota((rows, every), 1)
    codes_t = codes.T
    takers = [as_bf16(place_t == slot_col + CAP)]
    given = lax.rem(place_t, slots) < CAP
    rank_t = lax.rem(place_t, CAP)
    for q in range(QB):
        hit = given & (codes_t == ((me * CAP + rank_t) * QB + q).astype(F32))
        hit = jnp.where(hit, F32(1), F32(0))
        folded = sum(hit[b * samples : (b + 1) * samples] for b in range(GB))
        takers.append(folded.astype(BF16))
    takers = jnp.concatenate(takers, 0)

    lax.fori_loop(chunks // 2, chunks, element_chunk, 0)

    lower_out[...] = acc[:samples, edges:extended] + acc[samples : 2 * samples, edges:extended]
    lower_copy = pltpu.make_async_remote_copy(
        src_ref=lower_out,
        dst_ref=lower_in,
        send_sem=lower_send,
        recv_sem=lower_recv,
        device_id=(me, above),
        device_id_type=MESH,
    )
    lower_copy.start()

    def bulk(buf, sem):
        view = buf.at[pl.ds(0, (stators - 1) * slots), :]
        return pltpu.make_async_copy(view, view, sem)

    bulk(recvbuf, data_recv).wait()
    jumps = recvbuf[...] - jnp.where(wanted, 0.0, facing_rows)
    sums = add_halves(mul(takers, side_by_side(jumps)))
    rotor_term = PENALTY * (rotor - sums[:rows])
    stator_term = -PENALTY * dot3(sums[rows:], mortar[...], NT)
    for b in range(GB):
        lanes = pl.ds(rotor_start + b * GE, GE)
        acc[0:samples, lanes] += rotor_term[b * samples : (b + 1) * samples]
    for q in range(QB):
        lanes = pl.ds(face + q * GE, GE)
        acc[0:samples, lanes] += stator_term[q * samples : (q + 1) * samples]

    lower_copy.wait()
    linked = jnp.where(ax > 0, F32(1), F32(0))
    acc[0:samples, 0:face] += lower_in[...] * linked
    residual = acc[0:samples, 0:edges] + acc[samples : 2 * samples, 0:edges]
    adjoint[...] = table_dot(table_t[...], residual)

    bulk(meta, meta_send).wait()
    bulk(sendbuf, data_send).wait()


def on_device(coeffs, elem_edge, curl_map, jacobian, flux_fwd, density, mortar, gap_peer, gap_block):
    stators, axials = lax.axis_size("stator"), lax.axis_size("axial")
    samples, edges = coeffs.shape
    elements = elem_edge.shape[1]
    face = edges // 8
    rows = samples * GB
    every = stators * 2 * CAP
    table = dft_table(samples)
    packed = gap_peer.reshape(1, rows) * QB + gap_block.reshape(1, rows)
    vmem = pl.BlockSpec(memory_space=pltpu.VMEM)
    adjoint, grad = pl.pallas_call(
        functools.partial(kernel, stators, axials),
        out_shape=(
            jax.ShapeDtypeStruct((samples, edges), F32),
            jax.ShapeDtypeStruct((1, elements), F32),
        ),
        in_specs=[vmem] * 10,
        out_specs=(vmem, vmem),
        scratch_shapes=[
            pltpu.VMEM((samples, face), F32),
            pltpu.VMEM((samples, face), F32),
            pltpu.VMEM((samples, face), F32),
            pltpu.VMEM((every, rows), F32),
            pltpu.VMEM((every, GE), F32),
            pltpu.VMEM((every, GE), F32),
            pltpu.VMEM((samples * QB, GE), F32),
            pltpu.VMEM((samples, edges), F32),
            pltpu.VMEM((2 * samples, edges + face), BF16),
            pltpu.VMEM((edges + face, 6 * CHUNK), BF16),
            pltpu.VMEM((2 * samples, edges + face), F32),
        ]
        + [pltpu.SemaphoreType.DMA] * 8,
        compiler_params=pltpu.CompilerParams(
            collective_id=0, has_side_effects=True, vmem_limit_bytes=48 * 1024 * 1024
        ),
    )(
        coeffs,
        elem_edge,
        curl_map,
        jacobian,
        flux_fwd,
        density.reshape(1, elements),
        mortar,
        packed,
        jnp.asarray(triple(table)),
        jnp.asarray(triple(np.ascontiguousarray(table.T))),
    )
    return adjoint, grad.reshape(elements)


def solution(mesh):
    placed = (
        P(None, ("stator", "axial")),
        P(None, ("stator", "axial")),
        P(None, None, ("stator", "axial")),
        P(None, None, ("stator", "axial")),
        P(None, None, ("stator", "axial")),
        P(("stator", "axial")),
        P(),
        P(("stator", "axial"), None),
        P(("stator", "axial")),
    )
    return jax.shard_map(
        on_device,
        mesh=mesh,
        in_specs=placed,
        out_specs=(P(None, ("stator", "axial")), P(("stator", "axial"))),
        check_vma=False,
    )
```

time: 266 us -> 42.1 us (0.16); the launches traced: 261 us -> 41.7 us
  waiting for transfers between devices: 140 us -> 0 us
  other arithmetic: 43.1 us -> 0.01 us
  Pallas kernels: 0 us -> 31.7 us
  matrix products: 25.5 us -> 0 us
  local copies, waits for them, and re-layouts: 32.7 us -> 9.3 us
  between operations: 14.3 us -> 0.67 us
  starting transfers between devices: 5.95 us -> 0 us
    reduce_scatter x1 -> x0, waiting for transfers between devices: 140 us -> none  [on_device(): lax.psum_scatter(jump_sums, 'stator', scatter_dimension=0, tiled=True)]
    scatter-add x4 -> x0, other arithmetic: 37.6 us -> none  [the longest x1 33.8 us: element_work(): jax.ops.segment_sum(element_terms.reshape(-1, samples), elem_edge.reshape...]
    pallas_call x0 -> x1, Pallas kernels: none -> 31.7 us  [on_device(): pl.pallas_call(functools.partial(kernel, stators, axials), out_shape=(jax...]
    dot_general x6 -> x0, matrix products: 25.5 us -> none  [the longest x1 11.4 us: element_work(): jnp.einsum('cke,ske->cse', curl_map, values, precision=lax.Precision.HIGH...]
    gather x3 -> x0, local copies, waits for them, and re-layouts: 23.1 us -> none  [the longest x1 20.9 us: element_work(): values = extended[:, elem_edge]]
    unnamed x13 -> x24, local copies, waits for them, and re-layouts: 1.7 us -> 9.3 us
    ppermute x2 -> x0, starting transfers between devices: 5.87 us -> none  [shifted(): lax.ppermute(value, axis, [(source, source + steps) for source in range(l...]
    another operation x3 -> x0, local copies, waits for them, and re-layouts: 3.15 us -> none  [the longest x1 1.77 us: element_work(): jnp.stack([jac[0] * flux_lam[0] + jac[3] * flux_lam[1] + jac[4] * flux_la...]
  transfers between devices with their start and end apart: 4 -> 0, of which waited for: 2 -> 0; matrix products, arithmetic and copies ran while one was open for 35% -> 0% of each run, Pallas kernels for 0% -> 0%
where the time goes in v1:
time: 42.1 us; the launch traced here: 41.7 us
  Pallas kernels  31.7 us (75%)
  local copies, waits for them, and re-layouts  9.3 us (22%)
  between operations  0.67 us (2%)
    pallas_call x1, Pallas kernels, on_device(): pl.pallas_call(functools.partial(kernel, stators, axials), out_shape=(jax...  31.7 us
    unnamed x24, local copies, waits for them, and re-layouts  9.3 us

profile of v1, /device:TPU:1, one launch (start us, length us, event | category | flops | bytes accessed | tf_op | source)
XLA Modules:
  0.0 41.7 jit_solution(3660172134851252447)
XLA Ops:
  0.6 0.0 copy-start.9
  0.6 0.0 copy-start.10
  0.6 0.6 %copy-done.9 = s32[128]{0:T(128)S(1)} copy-done((s32[128]{0:T(128)S(1)}, s32[128]{0:T(128)}, u32[]{:S(2)}) %copy-start.9) | copy-done | bytes 536
  1.3 0.0 copy-done.10
  1.3 0.0 copy-start
  1.3 1.0 %copy-done = bf16[6,32,1024]{2,1,0:T(8,128)(2,1)S(1)} copy-done((bf16[6,32,1024]{2,1,0:T(8,128)(2,1)S(1)}, bf16[6,32,1024]{2,1,0:T(8,128)(2,1)}, u32[]{:S(2)}) %copy-start) | copy-done | bytes 393240
  2.3 0.0 copy-start.1
  2.3 0.9 %copy-done.1 = bf16[3,32,1024]{2,1,0:T(8,128)(2,1)S(1)} copy-done((bf16[3,32,1024]{2,1,0:T(8,128)(2,1)S(1)}, bf16[3,32,1024]{2,1,0:T(8,128)(2,1)}, u32[]{:S(2)}) %copy-start.1) | copy-done | bytes 196632
  3.2 0.0 copy-start.2
  3.2 0.9 %copy-done.2 = f32[32,1024]{1,0:T(8,128)S(1)} copy-done((f32[32,1024]{1,0:T(8,128)S(1)}, f32[32,1024]{1,0:T(8,128)}, u32[]{:S(2)}) %copy-start.2) | copy-done | bytes 131096
  4.1 0.0 copy-start.3
  4.1 0.9 %copy-done.3 = f32[3,6,1024]{2,1,0:T(8,128)S(1)} copy-done((f32[3,6,1024]{2,1,0:T(8,128)S(1)}, f32[3,6,1024]{2,1,0:T(8,128)}, u32[]{:S(2)}) %copy-start.3) | copy-done | bytes 73752
  5.0 0.0 copy-start.4
  5.0 0.8 %copy-done.4 = f32[128,128]{1,0:T(8,128)S(1)} copy-done((f32[128,128]{1,0:T(8,128)S(1)}, f32[128,128]{1,0:T(8,128)}, u32[]{:S(2)}) %copy-start.4) | copy-done | bytes 65560
  5.9 0.0 copy-start.5
  5.9 0.8 %copy-done.5 = s32[6,1024]{1,0:T(8,128)S(1)} copy-done((s32[6,1024]{1,0:T(8,128)S(1)}, s32[6,1024]{1,0:T(8,128)}, u32[]{:S(2)}) %copy-start.5) | copy-done | bytes 24600
  6.6 0.0 copy-start.6
  6.6 0.7 %copy-done.6 = bf16[32,96]{1,0:T(8,128)(2,1)S(1)} copy-done((bf16[32,96]{1,0:T(8,128)(2,1)S(1)}, bf16[32,96]{1,0:T(8,128)(2,1)}, u32[]{:S(2)}) %copy-start.6) | copy-done | bytes 6168
  7.3 0.0 copy-start.7
  7.3 0.7 %copy-done.7 = bf16[32,96]{1,0:T(8,128)(2,1)S(1)} copy-done((bf16[32,96]{1,0:T(8,128)(2,1)S(1)}, bf16[32,96]{1,0:T(8,128)(2,1)}, u32[]{:S(2)}) %copy-start.7) | copy-done | bytes 6168
  8.0 0.0 copy-start.8
  8.0 0.7 %copy-done.8 = f32[1024]{0:T(1024)S(1)} copy-done((f32[1024]{0:T(1024)S(1)}, f32[1024]{0:T(1024)}, u32[]{:S(2)}) %copy-start.8) | copy-done | bytes 4120
  8.7 31.7 %shard_map.122 = (f32[32,1024]{1,0:T(8,128)S(1)}, f32[1,1024]{1,0:T(1,128)S(1)}) custom-call(f32[32,1024]{1,0:T(8,128)S(1)} %copy-done.2, s32[6,1024]{1,0:T(8,128)S(1)} %copy-done.5, f32[3,6,1024]{2,1,0:T(8,128)S(1)} %copy-done.3, bf16[6,32,1024]{2,1,0:T(8,128)(2,1)S(1)} %copy-done, bf16[3,32,1024]{2,1,0:T(8,128)(2,1)S(1)} %copy-done.1, ...), custom_call_target="tpu_custom_call" | custom-call | tf_op jit(solution)/shard_map/pallas_call | solution.py:332
  40.4 0.7 %copy.15 = f32[32,1024]{1,0:T(8,128)} copy(f32[32,1024]{1,0:T(8,128)S(1)} %get-tuple-element.8) | data formatting | bytes 262144
  41.1 0.6 %copy.16 = f32[1024]{0:T(1024)} copy(f32[1024]{0:T(1024)S(1)} %bitcast.9) | data formatting | bytes 8192
  (1 shorter events, 0.0 us)
Async XLA Ops:
  0.6 0.7 %copy-start.9 = (s32[128]{0:T(128)S(1)}, s32[128]{0:T(128)}, u32[]{:S(2)}) copy-start(s32[128]{0:T(128)} %param.19) | copy-start | bytes 1540
  0.6 0.7 %copy-start.10 = (s32[128,1]{0,1:T(1,128)S(1)}, s32[128,1]{0,1:T(1,128)}, u32[]{:S(2)}) copy-start(s32[128,1]{0,1:T(1,128)} %param.18) | copy-start | bytes 1540
  1.3 1.0 %copy-start = (bf16[6,32,1024]{2,1,0:T(8,128)(2,1)S(1)}, bf16[6,32,1024]{2,1,0:T(8,128)(2,1)}, u32[]{:S(2)}) copy-start(bf16[6,32,1024]{2,1,0:T(8,128)(2,1)} %jac.1) | copy-start | bytes 1179652
  2.3 0.9 %copy-start.1 = (bf16[3,32,1024]{2,1,0:T(8,128)(2,1)S(1)}, bf16[3,32,1024]{2,1,0:T(8,128)(2,1)}, u32[]{:S(2)}) copy-start(bf16[3,32,1024]{2,1,0:T(8,128)(2,1)} %fwd.1) | copy-start | bytes 589828
  3.2 0.9 %copy-start.2 = (f32[32,1024]{1,0:T(8,128)S(1)}, f32[32,1024]{1,0:T(8,128)}, u32[]{:S(2)}) copy-start(f32[32,1024]{1,0:T(8,128)} %coeffs.1) | copy-start | bytes 393220
  4.1 0.9 %copy-start.3 = (f32[3,6,1024]{2,1,0:T(8,128)S(1)}, f32[3,6,1024]{2,1,0:T(8,128)}, u32[]{:S(2)}) copy-start(f32[3,6,1024]{2,1,0:T(8,128)} %curl.1) | copy-start | bytes 221188
  5.0 0.8 %copy-start.4 = (f32[128,128]{1,0:T(8,128)S(1)}, f32[128,128]{1,0:T(8,128)}, u32[]{:S(2)}) copy-start(f32[128,128]{1,0:T(8,128)} %mortar.1) | copy-start | bytes 196612
  5.9 0.8 %copy-start.5 = (s32[6,1024]{1,0:T(8,128)S(1)}, s32[6,1024]{1,0:T(8,128)}, u32[]{:S(2)}) copy-start(s32[6,1024]{1,0:T(8,128)} %edge.1) | copy-start | bytes 73732
  6.6 0.7 %copy-start.6 = (bf16[32,96]{1,0:T(8,128)(2,1)S(1)}, bf16[32,96]{1,0:T(8,128)(2,1)}, u32[]{:S(2)}) copy-start(bf16[32,96]{1,0:T(8,128)(2,1)} %constant.7.clone.table_t) | copy-start | bytes 18436
  7.3 0.7 %copy-start.7 = (bf16[32,96]{1,0:T(8,128)(2,1)S(1)}, bf16[32,96]{1,0:T(8,128)(2,1)}, u32[]{:S(2)}) copy-start(bf16[32,96]{1,0:T(8,128)(2,1)} %constant.6.clone.table) | copy-start | bytes 18436
  8.0 0.7 %copy-start.8 = (f32[1024]{0:T(1024)S(1)}, f32[1024]{0:T(1024)}, u32[]{:S(2)}) copy-start(f32[1024]{0:T(1024)} %param.16) | copy-start | bytes 12292

commit v2 on v1

v2 whole, which is shorter than its diff:
```python
import functools
import math

import jax
import jax.numpy as jnp
import numpy as np
from jax import lax
from jax.experimental import pallas as pl
from jax.experimental.pallas import tpu as pltpu
from jax.sharding import PartitionSpec as P

GE = 128
GB = 4
QB = 2
CAP = 4
PENALTY = 4.0
SIMP_POWER = 3.0
CHUNK = 256
GROUP = 8

MESH = pl.DeviceIdType.MESH
F32 = jnp.float32
BF16 = jnp.bfloat16
NN = (((1,), (0,)), ((), ()))
NT = (((1,), (1,)), ((), ()))


def dft_table(count):
    rows = np.arange(count, dtype=np.float64)[:, None]
    index = np.arange(count)
    harmonic = ((index + 1) // 2).astype(np.float64)[None, :]
    is_sine = ((index % 2 == 0) & (index > 0))[None, :]
    angle = 2.0 * math.pi * harmonic * rows / count
    table = np.where(is_sine, np.sin(angle), np.cos(angle))
    return (table * math.sqrt(2.0 / count)).astype(np.float32)


def triple(table):
    high = table.astype(jnp.bfloat16)
    low = (table - high.astype(np.float32)).astype(jnp.bfloat16)
    return np.concatenate([high, high, low], 1)


def split(value):
    high = value.astype(BF16)
    return high, (value - high.astype(F32)).astype(BF16)


def mul(a, b, dims=NN):
    return lax.dot_general(a, b, dims, preferred_element_type=F32)


def table_dot(table, value):
    high, low = split(value)
    return mul(table, jnp.concatenate([high, low, high], 0))


def dot3(a, b, dims=NN):
    a_high, a_low = split(a)
    b_high, b_low = split(b)
    return mul(a_high, b_high, dims) + mul(a_high, b_low, dims) + mul(a_low, b_high, dims)


def side_by_side(value):
    return jnp.concatenate(split(value), 1)


def add_halves(value):
    half = value.shape[1] // 2
    return value[:, :half] + value[:, half:]


def as_bf16(mask):
    return jnp.where(mask, F32(1), F32(0)).astype(BF16)


def iota(shape, dim):
    return lax.broadcasted_iota(jnp.int32, shape, dim)


def kernel(
    stators,
    axials,
    coeffs_hbm,
    edge_hbm,
    curl_hbm,
    jac_hbm,
    fwd_hbm,
    density_hbm,
    mortar_hbm,
    peers_hbm,
    blocks_hbm,
    table_hbm,
    table_t_hbm,
    adjoint_hbm,
    grad_hbm,
    coeffs,
    edge,
    curl,
    jac,
    fwd,
    density,
    mortar,
    peers,
    blocks,
    table,
    table_t,
    upper,
    lower_out,
    lower_in,
    code_own,
    codes,
    mapped,
    rotor_out,
    rotor_mid,
    rotor_in,
    reply_out,
    reply_in,
    ext,
    values,
    hot,
    acc,
    adjoint,
    grad,
    load,
    send,
    recv,
    store,
):
    samples, edges = coeffs.shape
    face = edges // 8
    extended = edges + face
    rows = samples * GB
    ring = stators // GROUP
    rotor_start = edges - GB * GE
    me, ax = lax.axis_index("stator"), lax.axis_index("axial")
    z, w = lax.div(me, GROUP), lax.rem(me, GROUP)
    above, below = lax.rem(ax + 1, axials), lax.rem(ax + axials - 1, axials)

    arrivals = []
    for index, (source, target) in enumerate(
        (
            (peers_hbm, peers),
            (blocks_hbm, blocks),
            (coeffs_hbm, coeffs),
            (table_hbm, table),
            (mortar_hbm, mortar),
            (edge_hbm, edge),
            (curl_hbm, curl),
            (jac_hbm, jac),
            (fwd_hbm, fwd),
            (density_hbm, density),
            (table_t_hbm, table_t),
        )
    ):
        arrivals.append(pltpu.make_async_copy(source, target, load.at[index]))
        arrivals[-1].start()

    along_z = sorted(range(1, ring), key=lambda step: -min(step, ring - step))
    along_w = sorted(range(1, GROUP), key=lambda step: -min(step, GROUP - step))
    z_peers = [lax.rem(z + step, ring) for step in along_z]
    w_peers = [lax.rem(w + step, GROUP) for step in along_w]

    barrier = pltpu.get_barrier_semaphore()

    def greet(stator, axial):
        pl.semaphore_signal(barrier, inc=1, device_id=(stator, axial), device_id_type=MESH)

    for other in z_peers:
        greet(other * GROUP + w, ax)
    for other in w_peers:
        greet(z * GROUP + other, ax)
    for other in (above, below):
        greet(me, other)

    def push(source, target, index, stator, axial):
        copy = pltpu.make_async_remote_copy(
            src_ref=source,
            dst_ref=target,
            send_sem=send.at[index],
            recv_sem=recv.at[index],
            device_id=(stator, axial),
            device_id_type=MESH,
        )
        copy.start()
        return copy

    def await_bytes(view, sem):
        pltpu.make_async_copy(view, view, sem).wait()

    arrivals[0].wait()
    arrivals[1].wait()
    a, b = iota((rows, rows), 0), iota((rows, rows), 1)
    own_order = b == lax.rem(a, samples) * GB + lax.div(a, samples)
    listed = (peers[...] * QB + blocks[...]).astype(F32)
    col = jnp.sum(jnp.where(own_order, listed, 0.0), axis=1, keepdims=True)
    row = jnp.sum(jnp.where(a == b, col, 0.0), axis=0, keepdims=True)
    peer_col, peer_row = jnp.floor(col * 0.5), jnp.floor(row * 0.5)
    same = peer_col == peer_row
    rank_row = jnp.sum(jnp.where(same & (a < b), 1.0, 0.0), axis=0, keepdims=True)
    rank_col = jnp.sum(jnp.where(same & (b < a), 1.0, 0.0), axis=1, keepdims=True)

    def slot(peer, rank):
        ring_place = jnp.floor(peer * (1.0 / GROUP))
        group_place = peer - GROUP * ring_place
        return (group_place * (ring * CAP) + ring_place * CAP + rank).astype(jnp.int32)

    slot_row, slot_col = slot(peer_row, rank_row), slot(peer_col, rank_col)
    code_row = (peer_row * CAP + rank_row) * QB + (row - 2.0 * peer_row)
    code_own[...] = jnp.broadcast_to(code_row, (CAP, rows))

    arrivals[2].wait()
    arrivals[3].wait()
    arrivals[4].wait()
    own = table_dot(table[...], coeffs[...])
    ext[:, 0:edges] = own
    slots = stators * CAP
    rotor = jnp.concatenate(
        [own[:, rotor_start + b * GE : rotor_start + (b + 1) * GE] for b in range(GB)], 0
    )
    placed = as_bf16(iota((slots, rows), 0) == slot_row)
    rotor_out[...] = add_halves(mul(placed, side_by_side(rotor))).reshape(rotor_out.shape)
    faces = jnp.concatenate(
        [own[:, face + q * GE : face + (q + 1) * GE] for q in range(QB)], 0
    )
    own_mapped = dot3(faces, mortar[...])
    mapped[w] = own_mapped

    pl.semaphore_wait(barrier, (ring - 1) + (GROUP - 1) + 2)

    upper_copy = push(coeffs.at[:, pl.ds(0, face)], upper, 0, me, below)
    at_me = pl.ds(z * CAP, CAP)
    for other in z_peers:
        push(code_own, codes.at[w, at_me], 1, other * GROUP + w, ax)
    pltpu.make_async_copy(code_own, codes.at[w, at_me], recv.at[1]).start()
    for other in w_peers:
        push(mapped.at[w], mapped.at[w], 2, z * GROUP + other, ax)
    for other in z_peers:
        push(
            rotor_out.at[:, pl.ds(other * CAP, CAP)],
            rotor_mid.at[:, at_me],
            3,
            other * GROUP + w,
            ax,
        )
    pltpu.make_async_copy(rotor_out.at[:, at_me], rotor_mid.at[:, at_me], recv.at[3]).start()

    arrivals[5].wait()

    def pick(lanes, m):
        named = jnp.broadcast_to(edge[m : m + 1, lanes], (samples, GE))
        return named & (GE - 1), lax.shift_right_logical(named, GE.bit_length() - 1)

    def gather_own(part, carry):
        lanes = pl.ds(pl.multiple_of(part * GE, GE), GE)
        for m in range(6):
            low, high = pick(lanes, m)
            found = None
            for k in range(edges // GE):
                here = jnp.take_along_axis(ext[:, k * GE : (k + 1) * GE], low, axis=1)
                found = here if found is None else jnp.where(high == k, here, found)
            values[m, :, lanes] = found
        return carry

    lax.fori_loop(0, edges // GE, gather_own, 0)

    upper_copy.wait_recv()
    inside = jnp.where(ax < axials - 1, F32(1), F32(0))
    ext[:, edges:extended] = table_dot(table[...], upper[...] * inside)
    for index in range(6, 10):
        arrivals[index].wait()
    acc[...] = jnp.zeros_like(acc)

    def element_chunk(chunk, carry):
        lanes = pl.ds(pl.multiple_of(chunk * CHUNK, CHUNK), CHUNK)
        sub = iota((extended, CHUNK), 0).astype(jnp.int16)
        named = edge[:, lanes].astype(jnp.int16)
        for m in range(6):
            mask = sub == named[m : m + 1, :]
            hot[:, m * CHUNK : (m + 1) * CHUNK] = jnp.where(mask, BF16(1), BF16(0))
        found = []
        for m in range(6):
            pieces = []
            for part in range(CHUNK // GE):
                here = pl.ds(pl.multiple_of(chunk * CHUNK + part * GE, GE), GE)
                low, high = pick(here, m)
                rim = jnp.take_along_axis(ext[:, edges:extended], low, axis=1)
                pieces.append(jnp.where(high == edges // GE, rim, values[m, :, here]))
            found.append(jnp.concatenate(pieces, 1))
        maps = curl[:, :, lanes]
        flux = [sum(maps[c, m : m + 1, :] * found[m] for m in range(6)) for c in range(3)]
        j = [jac[k, :, lanes].astype(F32) for k in range(6)]
        field = [
            j[0] * flux[0] + j[3] * flux[1] + j[4] * flux[2],
            j[3] * flux[0] + j[1] * flux[1] + j[5] * flux[2],
            j[4] * flux[0] + j[5] * flux[1] + j[2] * flux[2],
        ]
        energy = sum(flux[c] * fwd[c, :, lanes].astype(F32) for c in range(3))
        energy = jnp.sum(energy, axis=0, keepdims=True)
        dens = density[:, lanes]
        grad[:, lanes] = SIMP_POWER * dens * dens * energy / samples
        highs, lows = [], []
        for m in range(6):
            high, low = split(sum(maps[c, m : m + 1, :] * field[c] for c in range(3)))
            highs.append(high)
            lows.append(low)
        terms = jnp.concatenate([jnp.concatenate(highs, 1), jnp.concatenate(lows, 1)], 0)
        acc[...] += mul(hot[...], terms, NT)
        return carry

    lax.fori_loop(0, edges // CHUNK, element_chunk, 0)
    kept = [pltpu.make_async_copy(grad, grad_hbm, store.at[0])]
    kept[0].start()
    sums = acc[...].T
    sums = sums[:samples] + sums[samples : 2 * samples]
    lower_out[...] = sums[:, edges:extended]
    lower_copy = push(lower_out, lower_in, 4, me, above)

    await_bytes(codes.at[w], recv.at[1])
    for other in w_peers:
        push(codes.at[w], codes.at[w], 5, z * GROUP + other, ax)
    await_bytes(mapped.at[pl.ds(0, GROUP - 1)], recv.at[2])
    asked = codes[w]
    rank = lax.rem(iota((ring * CAP, rows), 0), CAP)

    def by_row(value):
        return jnp.concatenate([value] * GB, 0)

    for other in range(GROUP):
        hits = [
            as_bf16(asked == (((z * GROUP + other) * CAP + rank) * QB + q).astype(F32))
            for q in range(QB)
        ]
        source = [by_row(mapped[other, q * samples : (q + 1) * samples]) for q in range(QB)]
        reply_out[other] = add_halves(
            mul(jnp.concatenate(hits, 1), side_by_side(jnp.concatenate(source, 0)))
        )
    for other in z_peers:
        push(
            reply_out.at[:, pl.ds(other * CAP, CAP)],
            reply_in.at[:, at_me],
            6,
            other * GROUP + w,
            ax,
        )
    pltpu.make_async_copy(reply_out.at[:, at_me], reply_in.at[:, at_me], recv.at[6]).start()

    await_bytes(rotor_mid, recv.at[3])
    for other in w_peers:
        push(rotor_mid.at[other], rotor_in.at[w], 7, z * GROUP + other, ax)
    rotor_in[w] = rotor_mid[w]
    await_bytes(codes.at[pl.ds(0, GROUP - 1)], recv.at[5])
    listed_t = codes[...].reshape(slots, rows).T
    rank_t = lax.rem(iota((rows, slots), 1), CAP)
    takers, counts = [], []
    for q in range(QB):
        hit = listed_t == ((me * CAP + rank_t) * QB + q).astype(F32)
        hit = jnp.where(hit, F32(1), F32(0))
        folded = sum(hit[b * samples : (b + 1) * samples] for b in range(GB))
        takers.append(folded.astype(BF16))
        counts.append(jnp.sum(folded, axis=1, keepdims=True))
    takers, counts = jnp.concatenate(takers, 0), jnp.concatenate(counts, 0)
    await_bytes(rotor_in.at[pl.ds(0, GROUP - 1)], recv.at[7])
    arrived = add_halves(mul(takers, side_by_side(rotor_in[...].reshape(slots, GE))))
    stator_term = -PENALTY * dot3(arrived - counts * mapped[w], mortar[...], NT)

    arrivals[10].wait()
    lower_copy.wait_recv()
    linked = jnp.where(ax > 0, F32(1), F32(0))
    residual = [sums[:, 0:face] + lower_in[...] * linked]
    for q in range(QB):
        here = sums[:, face + q * GE : face + (q + 1) * GE]
        residual.append(here + stator_term[q * samples : (q + 1) * samples])
    residual.append(sums[:, face + QB * GE : rotor_start])
    adjoint[:, 0:rotor_start] = table_dot(table_t[...], jnp.concatenate(residual, 1))
    first, last = pl.ds(0, rotor_start), pl.ds(rotor_start, edges - rotor_start)
    kept.append(
        pltpu.make_async_copy(adjoint.at[:, first], adjoint_hbm.at[:, first], store.at[1])
    )
    kept[1].start()

    chosen = as_bf16(iota((rows, slots), 1) == slot_col)
    await_bytes(reply_in, recv.at[6])
    facing = add_halves(mul(chosen, side_by_side(reply_in[...].reshape(slots, GE))))
    jumps = rotor - facing
    residual = [
        sums[:, rotor_start + b * GE : rotor_start + (b + 1) * GE]
        + PENALTY * jumps[b * samples : (b + 1) * samples]
        for b in range(GB)
    ]
    adjoint[:, rotor_start:edges] = table_dot(table_t[...], jnp.concatenate(residual, 1))

    kept.append(pltpu.make_async_copy(adjoint.at[:, last], adjoint_hbm.at[:, last], store.at[2]))
    kept[2].start()

    upper_copy.wait_send()
    lower_copy.wait_send()
    await_bytes(codes.at[0, pl.ds(0, (ring - 1) * CAP)], send.at[1])
    await_bytes(mapped.at[pl.ds(0, GROUP - 1)], send.at[2])
    await_bytes(rotor_mid.at[:, pl.ds(0, (ring - 1) * CAP)], send.at[3])
    await_bytes(codes.at[pl.ds(0, GROUP - 1)], send.at[5])
    await_bytes(reply_out.at[:, pl.ds(0, (ring - 1) * CAP)], send.at[6])
    await_bytes(rotor_in.at[pl.ds(0, GROUP - 1)], send.at[7])
    for copy in kept:
        copy.wait()


def flush(a, b, c, d):
    c[...] = a[...]
    d[...] = b[...]


def on_device(coeffs, elem_edge, curl_map, jacobian, flux_fwd, density, mortar, gap_peer, gap_block):
    stators, axials = lax.axis_size("stator"), lax.axis_size("axial")
    samples, edges = coeffs.shape
    elements = elem_edge.shape[1]
    face = edges // 8
    rows = samples * GB
    ring = stators // GROUP
    table = dft_table(samples)
    operands = (
        coeffs,
        elem_edge,
        curl_map,
        jacobian,
        flux_fwd,
        density.reshape(1, elements),
        mortar,
        gap_peer.reshape(1, rows),
        gap_block.reshape(1, rows),
        jnp.asarray(triple(table)),
        jnp.asarray(triple(np.ascontiguousarray(table.T))),
    )
    hbm = pl.BlockSpec(memory_space=pltpu.HBM)
    shapes = (
        jax.ShapeDtypeStruct((samples, edges), F32),
        jax.ShapeDtypeStruct((1, elements), F32),
    )
    strip = pltpu.VMEM((samples, face), F32)
    slotted = pltpu.VMEM((GROUP, ring * CAP, GE), F32)
    adjoint, grad = pl.pallas_call(
        functools.partial(kernel, stators, axials),
        out_shape=shapes,
        in_specs=[hbm] * len(operands),
        out_specs=(hbm, hbm),
        scratch_shapes=[pltpu.VMEM(operand.shape, operand.dtype) for operand in operands]
        + [
            strip,
            strip,
            strip,
            pltpu.VMEM((CAP, rows), F32),
            pltpu.VMEM((GROUP, ring * CAP, rows), F32),
            pltpu.VMEM((GROUP, samples * QB, GE), F32),
            slotted,
            slotted,
            slotted,
            slotted,
            slotted,
            pltpu.VMEM((samples, edges + face), F32),
            pltpu.VMEM((6, samples, elements), F32),
            pltpu.VMEM((edges + face, 6 * CHUNK), BF16),
            pltpu.VMEM((edges + face, 2 * samples), F32),
            pltpu.VMEM((samples, edges), F32),
            pltpu.VMEM((1, elements), F32),
            pltpu.SemaphoreType.DMA((len(operands),)),
            pltpu.SemaphoreType.DMA((8,)),
            pltpu.SemaphoreType.DMA((8,)),
            pltpu.SemaphoreType.DMA((3,)),
        ],
        compiler_params=pltpu.CompilerParams(
            collective_id=0, has_side_effects=True, vmem_limit_bytes=56 * 1024 * 1024
        ),
    )(*operands)
    vmem = pl.BlockSpec(memory_space=pltpu.VMEM)
    adjoint, grad = pl.pallas_call(flush, out_shape=shapes, in_specs=[vmem, vmem], out_specs=(vmem, vmem))(adjoint, grad)
    return adjoint, grad.reshape(elements)


def solution(mesh):
    placed = (
        P(None, ("stator", "axial")),
        P(None, ("stator", "axial")),
        P(None, None, ("stator", "axial")),
        P(None, None, ("stator", "axial")),
        P(None, None, ("stator", "axial")),
        P(("stator", "axial")),
        P(),
        P(("stator", "axial"), None),
        P(("stator", "axial")),
    )
    return jax.shard_map(
        on_device,
        mesh=mesh,
        in_specs=placed,
        out_specs=(P(None, ("stator", "axial")), P(("stator", "axial"))),
        check_vma=False,
    )
```

time: 42.1 us -> 27 us (0.64)
  local copies, waits for them, and re-layouts: 9.3 us -> 0 us
  Pallas kernels: 31.7 us -> 26.3 us
    unnamed x24 -> x0, local copies, waits for them, and re-layouts: 9.3 us -> none
    pallas_call x1 -> x2, Pallas kernels: 31.7 us -> 26.3 us  [the longest x1 24.7 us: on_device(): pl.pallas_call(functools.partial(kernel, stators, axials), out_shape=shap...]
where the time goes in v2:
time: 27 us; the launch traced here: 26.9 us
  Pallas kernels  26.3 us (97%)
  between operations  0.64 us (2%)
    pallas_call x1, Pallas kernels, on_device(): pl.pallas_call(functools.partial(kernel, stators, axials), out_shape=shap...  24.7 us
    pallas_call x1, Pallas kernels, on_device(): pl.pallas_call(flush, out_shape=shapes, in_specs=[vmem, vmem], out_specs=...  1.57 us

profile of v2, /device:TPU:1, one launch (start us, length us, event | category | flops | bytes accessed | tf_op | source)
XLA Modules:
  0.0 26.9 jit_solution(7395208725511586352)
XLA Ops:
  0.6 24.7 %shard_map.122 = (f32[32,1024]{1,0:T(8,128)}, f32[1,1024]{1,0:T(1,128)}) custom-call(f32[32,1024]{1,0:T(8,128)} %coeffs_hbm.1, s32[6,1024]{1,0:T(8,128)} %edge_hbm.1, f32[3,6,1024]{2,1,0:T(8,128)} %curl_hbm.1, bf16[6,32,1024]{2,1,0:T(8,128)(2,1)} %jac_hbm.1, bf16[3,32,1024]{2,1,0:T(8,128)(2,1)} %fwd_hbm.1, f32[1,1024]{1,0:T(1,128)} %bitcast.4, ...), custom_call_target="tpu_custom_call" | custom-call | tf_op jit(solution)/shard_map/pallas_call | solution.py:441
  25.3 1.6 %shard_map.123 = (f32[32,1024]{1,0:T(8,128)}, f32[1,1024]{1,0:T(1,128)}) custom-call(f32[32,1024]{1,0:T(8,128)} %get-tuple-element.6.a, f32[1,1024]{1,0:T(1,128)} %get-tuple-element.7.b), custom_call_target="tpu_custom_call" | custom-call | tf_op jit(solution)/shard_map/pallas_call | solution.py:475

commit v3 on v2

--- a/solution.py
+++ b/solution.py
@@ -16,6 +16,7 @@
 PENALTY = 4.0
 SIMP_POWER = 3.0
 CHUNK = 256
+EARLY = 2
 GROUP = 8
 
 MESH = pl.DeviceIdType.MESH
@@ -39,6 +40,13 @@
     high = table.astype(jnp.bfloat16)
     low = (table - high.astype(np.float32)).astype(jnp.bfloat16)
     return np.concatenate([high, high, low], 1)
+
+
+def back_table(table):
+    scaled = np.kron(np.eye(GB, dtype=np.float32), -PENALTY * table.T).astype(np.float32)
+    high = scaled.astype(jnp.bfloat16)
+    low = (scaled - high.astype(np.float32)).astype(jnp.bfloat16)
+    return np.concatenate([high, low], 0)
 
 
 def split(value):
@@ -92,8 +100,9 @@
     blocks_hbm,
     table_hbm,
     table_t_hbm,
-    adjoint_hbm,
-    grad_hbm,
+    back_hbm,
+    adjoint,
+    grad,
     coeffs,
     edge,
     curl,
@@ -105,6 +114,7 @@
     blocks,
     table,
     table_t,
+    back,
     upper,
     lower_out,
     lower_in,
@@ -118,14 +128,10 @@
     reply_in,
     ext,
     values,
-    hot,
     acc,
-    adjoint,
-    grad,
     load,
     send,
     recv,
-    store,
 ):
     samples, edges = coeffs.shape
     face = edges // 8
@@ -151,6 +157,7 @@
             (fwd_hbm, fwd),
             (density_hbm, density),
             (table_t_hbm, table_t),
+            (back_hbm, back),
         )
     ):
         arrivals.append(pltpu.make_async_copy(source, target, load.at[index]))
@@ -273,11 +280,6 @@
 
     def element_chunk(chunk, carry):
         lanes = pl.ds(pl.multiple_of(chunk * CHUNK, CHUNK), CHUNK)
-        sub = iota((extended, CHUNK), 0).astype(jnp.int16)
-        named = edge[:, lanes].astype(jnp.int16)
-        for m in range(6):
-            mask = sub == named[m : m + 1, :]
-            hot[:, m * CHUNK : (m + 1) * CHUNK] = jnp.where(mask, BF16(1), BF16(0))
         found = []
         for m in range(6):
             pieces = []
@@ -299,22 +301,27 @@
         energy = jnp.sum(energy, axis=0, keepdims=True)
         dens = density[:, lanes]
         grad[:, lanes] = SIMP_POWER * dens * dens * energy / samples
-        highs, lows = [], []
+        sub = iota((GE, CHUNK), 0).astype(jnp.int16)
+        none = jnp.zeros((2 * samples, CHUNK), BF16)
+        terms, hot = [], []
         for m in range(6):
-            high, low = split(sum(maps[c, m : m + 1, :] * field[c] for c in range(3)))
-            highs.append(high)
-            lows.append(low)
-        terms = jnp.concatenate([jnp.concatenate(highs, 1), jnp.concatenate(lows, 1)], 0)
-        acc[...] += mul(hot[...], terms, NT)
+            named = edge[m : m + 1, lanes]
+            low = (named & (GE - 1)).astype(jnp.int16)
+            high = lax.shift_right_logical(named, GE.bit_length() - 1)
+            high = jnp.broadcast_to(high, (2 * samples, CHUNK)).astype(jnp.int16)
+            hot.append(jnp.where(sub == low, BF16(1), BF16(0)))
+            term = sum(maps[c, m : m + 1, :] * field[c] for c in range(3))
+            term = jnp.concatenate(split(term), 0)
+            terms.append(
+                jnp.concatenate(
+                    [jnp.where(high == jnp.int16(k), term, none) for k in range(extended // GE)], 0
+                )
+            )
+        acc[...] += mul(jnp.concatenate(terms, 1), jnp.concatenate(hot, 1), NT)
         return carry
 
-    lax.fori_loop(0, edges // CHUNK, element_chunk, 0)
-    kept = [pltpu.make_async_copy(grad, grad_hbm, store.at[0])]
-    kept[0].start()
-    sums = acc[...].T
-    sums = sums[:samples] + sums[samples : 2 * samples]
-    lower_out[...] = sums[:, edges:extended]
-    lower_copy = push(lower_out, lower_in, 4, me, above)
+    chunks = edges // CHUNK
+    lax.fori_loop(0, EARLY, element_chunk, 0)
 
     await_bytes(codes.at[w], recv.at[1])
     for other in w_peers:
@@ -331,9 +338,10 @@
             as_bf16(asked == (((z * GROUP + other) * CAP + rank) * QB + q).astype(F32))
             for q in range(QB)
         ]
-        source = [by_row(mapped[other, q * samples : (q + 1) * samples]) for q in range(QB)]
+        source = side_by_side(mapped[other])
+        source = [by_row(source[q * samples : (q + 1) * samples]) for q in range(QB)]
         reply_out[other] = add_halves(
-            mul(jnp.concatenate(hits, 1), side_by_side(jnp.concatenate(source, 0)))
+            mul(jnp.concatenate(hits, 1), jnp.concatenate(source, 0))
         )
     for other in z_peers:
         push(
@@ -349,6 +357,14 @@
     for other in w_peers:
         push(rotor_mid.at[other], rotor_in.at[w], 7, z * GROUP + other, ax)
     rotor_in[w] = rotor_mid[w]
+
+    lax.fori_loop(EARLY, chunks, element_chunk, 0)
+    sums = acc[...].reshape(extended // GE, 2, samples, GE)
+    sums = sums[:, 0] + sums[:, 1]
+    sums = jnp.concatenate([sums[k] for k in range(extended // GE)], 1)
+    lower_out[...] = sums[:, edges:extended]
+    lower_copy = push(lower_out, lower_in, 4, me, above)
+
     await_bytes(codes.at[pl.ds(0, GROUP - 1)], recv.at[5])
     listed_t = codes[...].reshape(slots, rows).T
     rank_t = lax.rem(iota((rows, slots), 1), CAP)
@@ -373,25 +389,15 @@
         residual.append(here + stator_term[q * samples : (q + 1) * samples])
     residual.append(sums[:, face + QB * GE : rotor_start])
     adjoint[:, 0:rotor_start] = table_dot(table_t[...], jnp.concatenate(residual, 1))
-    first, last = pl.ds(0, rotor_start), pl.ds(rotor_start, edges - rotor_start)
-    kept.append(
-        pltpu.make_async_copy(adjoint.at[:, first], adjoint_hbm.at[:, first], store.at[1])
-    )
-    kept[1].start()
-
-    chosen = as_bf16(iota((rows, slots), 1) == slot_col)
-    await_bytes(reply_in, recv.at[6])
-    facing = add_halves(mul(chosen, side_by_side(reply_in[...].reshape(slots, GE))))
-    jumps = rotor - facing
-    residual = [
+    jumping = [
         sums[:, rotor_start + b * GE : rotor_start + (b + 1) * GE]
-        + PENALTY * jumps[b * samples : (b + 1) * samples]
+        + PENALTY * rotor[b * samples : (b + 1) * samples]
         for b in range(GB)
     ]
-    adjoint[:, rotor_start:edges] = table_dot(table_t[...], jnp.concatenate(residual, 1))
-
-    kept.append(pltpu.make_async_copy(adjoint.at[:, last], adjoint_hbm.at[:, last], store.at[2]))
-    kept[2].start()
+    base = table_dot(table_t[...], jnp.concatenate(jumping, 1))
+    arrivals[11].wait()
+    chosen = as_bf16(iota((rows, slots), 1) == slot_col)
+    chosen = mul(back[...], chosen).astype(BF16)
 
     upper_copy.wait_send()
     lower_copy.wait_send()
@@ -399,15 +405,28 @@
     await_bytes(mapped.at[pl.ds(0, GROUP - 1)], send.at[2])
     await_bytes(rotor_mid.at[:, pl.ds(0, (ring - 1) * CAP)], send.at[3])
     await_bytes(codes.at[pl.ds(0, GROUP - 1)], send.at[5])
+    await_bytes(rotor_in.at[pl.ds(0, GROUP - 1)], send.at[7])
+
+    await_bytes(reply_in, recv.at[6])
+    facing = mul(chosen, side_by_side(reply_in[...].reshape(slots, GE)))
+    facing = add_halves(facing[:rows]) + facing[rows:, :GE]
+    for b in range(GB):
+        lanes = slice(rotor_start + b * GE, rotor_start + (b + 1) * GE)
+        adjoint[:, lanes] = (
+            base[:, b * GE : (b + 1) * GE] + facing[b * samples : (b + 1) * samples]
+        )
     await_bytes(reply_out.at[:, pl.ds(0, (ring - 1) * CAP)], send.at[6])
-    await_bytes(rotor_in.at[pl.ds(0, GROUP - 1)], send.at[7])
-    for copy in kept:
+
+
+def flush(adjoint, grad, adjoint_hbm, grad_hbm, sems):
+    copies = (
+        pltpu.make_async_copy(adjoint, adjoint_hbm, sems.at[0]),
+        pltpu.make_async_copy(grad, grad_hbm, sems.at[1]),
+    )
+    for copy in copies:
+        copy.start()
+    for copy in copies:
         copy.wait()
-
-
-def flush(a, b, c, d):
-    c[...] = a[...]
-    d[...] = b[...]
 
 
 def on_device(coeffs, elem_edge, curl_map, jacobian, flux_fwd, density, mortar, gap_peer, gap_block):
@@ -430,7 +449,9 @@
         gap_block.reshape(1, rows),
         jnp.asarray(triple(table)),
         jnp.asarray(triple(np.ascontiguousarray(table.T))),
-    )
+        jnp.asarray(back_table(table)),
+    )
+    vmem = pl.BlockSpec(memory_space=pltpu.VMEM)
     hbm = pl.BlockSpec(memory_space=pltpu.HBM)
     shapes = (
         jax.ShapeDtypeStruct((samples, edges), F32),
@@ -438,11 +459,11 @@
     )
     strip = pltpu.VMEM((samples, face), F32)
     slotted = pltpu.VMEM((GROUP, ring * CAP, GE), F32)
-    adjoint, grad = pl.pallas_call(
+    results = pl.pallas_call(
         functools.partial(kernel, stators, axials),
         out_shape=shapes,
         in_specs=[hbm] * len(operands),
-        out_specs=(hbm, hbm),
+        out_specs=(vmem, vmem),
         scratch_shapes=[pltpu.VMEM(operand.shape, operand.dtype) for operand in operands]
         + [
             strip,
@@ -458,21 +479,22 @@
             slotted,
             pltpu.VMEM((samples, edges + face), F32),
             pltpu.VMEM((6, samples, elements), F32),
-            pltpu.VMEM((edges + face, 6 * CHUNK), BF16),
-            pltpu.VMEM((edges + face, 2 * samples), F32),
-            pltpu.VMEM((samples, edges), F32),
-            pltpu.VMEM((1, elements), F32),
+            pltpu.VMEM(((edges + face) // GE * 2 * samples, GE), F32),
             pltpu.SemaphoreType.DMA((len(operands),)),
             pltpu.SemaphoreType.DMA((8,)),
             pltpu.SemaphoreType.DMA((8,)),
-            pltpu.SemaphoreType.DMA((3,)),
         ],
         compiler_params=pltpu.CompilerParams(
-            collective_id=0, has_side_effects=True, vmem_limit_bytes=56 * 1024 * 1024
+            collective_id=0, has_side_effects=True, vmem_limit_bytes=32 * 1024 * 1024
         ),
-    )(*operands)
-    vmem = pl.BlockSpec(memory_space=pltpu.VMEM)
-    adjoint, grad = pl.pallas_call(flush, out_shape=shapes, in_specs=[vmem, vmem], out_specs=(vmem, vmem))(adjoint, grad)
+    )(*(pltpu.with_memory_space_constraint(operand, pltpu.HBM) for operand in operands))
+    adjoint, grad = pl.pallas_call(
+        flush,
+        out_shape=shapes,
+        in_specs=[vmem, vmem],
+        out_specs=(hbm, hbm),
+        scratch_shapes=[pltpu.SemaphoreType.DMA((2,))],
+    )(*(pltpu.with_memory_space_constraint(result, pltpu.VMEM) for result in results))
     return adjoint, grad.reshape(elements)
 
 

time: 27 us -> 22.7 us (0.84)
  Pallas kernels: 26.3 us -> 22 us
    pallas_call x1, Pallas kernels: 24.7 us -> 21.3 us  [on_device(): pl.pallas_call(functools.partial(kernel, stators, axials), out_shape=shap...]
    pallas_call x1, Pallas kernels: 1.57 us -> 0.68 us  [on_device(): pl.pallas_call(flush, out_shape=shapes, in_specs=[vmem, vmem], out_specs=...]
where the time goes in v3:
time: 22.7 us; the launch traced here: 22.6 us
  Pallas kernels  22 us (97%)
  between operations  0.64 us (3%)
    pallas_call x1, Pallas kernels, on_device(): pl.pallas_call(functools.partial(kernel, stators, axials), out_shape=shap...  21.3 us
    pallas_call x1, Pallas kernels, on_device(): pl.pallas_call(flush, out_shape=shapes, in_specs=[vmem, vmem], out_specs=...  0.68 us

profile of v3, /device:TPU:1, one launch (start us, length us, event | category | flops | bytes accessed | tf_op | source)
XLA Modules:
  0.0 22.6 jit_solution(17000366070495474845)
XLA Ops:
  0.6 21.3 %shard_map.131 = (f32[32,1024]{1,0:T(8,128)S(1)}, f32[1,1024]{1,0:T(1,128)S(1)}) custom-call(f32[32,1024]{1,0:T(8,128)} %coeffs_hbm.1, s32[6,1024]{1,0:T(8,128)} %edge_hbm.1, f32[3,6,1024]{2,1,0:T(8,128)} %curl_hbm.1, bf16[6,32,1024]{2,1,0:T(8,128)(2,1)} %jac_hbm.1, bf16[3,32,1024]{2,1,0:T(8,128)(2,1)} %fwd_hbm.1, f32[1,1024]{1,0:T(1,128)} %bitcast.4, ...), custom_call_target="tpu_custom_call" | custom-call | tf_op jit(solution)/shard_map/pallas_call | solution.py:462
  21.9 0.7 %shard_map.132 = (f32[32,1024]{1,0:T(8,128)}, f32[1,1024]{1,0:T(1,128)}) custom-call(f32[32,1024]{1,0:T(8,128)S(1)} %get-tuple-element.6.adjoint, f32[1,1024]{1,0:T(1,128)S(1)} %get-tuple-element.7.grad), custom_call_target="tpu_custom_call" | custom-call | tf_op jit(solution)/shard_map/pallas_call | solution.py:491

commit v4 on v3

--- a/solution.py
+++ b/solution.py
@@ -143,6 +143,23 @@
     z, w = lax.div(me, GROUP), lax.rem(me, GROUP)
     above, below = lax.rem(ax + 1, axials), lax.rem(ax + axials - 1, axials)
 
+    along_z = sorted(range(1, ring), key=lambda step: -min(step, ring - step))
+    along_w = sorted(range(1, GROUP), key=lambda step: -min(step, GROUP - step))
+    z_peers = [lax.rem(z + step, ring) for step in along_z]
+    w_peers = [lax.rem(w + step, GROUP) for step in along_w]
+
+    barrier = pltpu.get_barrier_semaphore()
+
+    def greet(stator, axial):
+        pl.semaphore_signal(barrier, inc=1, device_id=(stator, axial), device_id_type=MESH)
+
+    for other in z_peers:
+        greet(other * GROUP + w, ax)
+    for other in w_peers:
+        greet(z * GROUP + other, ax)
+    for other in (above, below):
+        greet(me, other)
+
     arrivals = []
     for index, (source, target) in enumerate(
         (
@@ -163,23 +180,6 @@
         arrivals.append(pltpu.make_async_copy(source, target, load.at[index]))
         arrivals[-1].start()
 
-    along_z = sorted(range(1, ring), key=lambda step: -min(step, ring - step))
-    along_w = sorted(range(1, GROUP), key=lambda step: -min(step, GROUP - step))
-    z_peers = [lax.rem(z + step, ring) for step in along_z]
-    w_peers = [lax.rem(w + step, GROUP) for step in along_w]
-
-    barrier = pltpu.get_barrier_semaphore()
-
-    def greet(stator, axial):
-        pl.semaphore_signal(barrier, inc=1, device_id=(stator, axial), device_id_type=MESH)
-
-    for other in z_peers:
-        greet(other * GROUP + w, ax)
-    for other in w_peers:
-        greet(z * GROUP + other, ax)
-    for other in (above, below):
-        greet(me, other)
-
     def push(source, target, index, stator, axial):
         copy = pltpu.make_async_remote_copy(
             src_ref=source,
@@ -195,6 +195,17 @@
     def await_bytes(view, sem):
         pltpu.make_async_copy(view, view, sem).wait()
 
+    arrivals[2].wait()
+    arrivals[3].wait()
+    arrivals[4].wait()
+    own = table_dot(table[...], coeffs[...])
+    ext[:, 0:edges] = own
+    faces = jnp.concatenate(
+        [own[:, face + q * GE : face + (q + 1) * GE] for q in range(QB)], 0
+    )
+    own_mapped = dot3(faces, mortar[...])
+    mapped[w] = own_mapped
+
     arrivals[0].wait()
     arrivals[1].wait()
     a, b = iota((rows, rows), 0), iota((rows, rows), 1)
@@ -216,30 +227,19 @@
     code_row = (peer_row * CAP + rank_row) * QB + (row - 2.0 * peer_row)
     code_own[...] = jnp.broadcast_to(code_row, (CAP, rows))
 
-    arrivals[2].wait()
-    arrivals[3].wait()
-    arrivals[4].wait()
-    own = table_dot(table[...], coeffs[...])
-    ext[:, 0:edges] = own
     slots = stators * CAP
     rotor = jnp.concatenate(
         [own[:, rotor_start + b * GE : rotor_start + (b + 1) * GE] for b in range(GB)], 0
     )
     placed = as_bf16(iota((slots, rows), 0) == slot_row)
     rotor_out[...] = add_halves(mul(placed, side_by_side(rotor))).reshape(rotor_out.shape)
-    faces = jnp.concatenate(
-        [own[:, face + q * GE : face + (q + 1) * GE] for q in range(QB)], 0
-    )
-    own_mapped = dot3(faces, mortar[...])
-    mapped[w] = own_mapped
-
     pl.semaphore_wait(barrier, (ring - 1) + (GROUP - 1) + 2)
 
-    upper_copy = push(coeffs.at[:, pl.ds(0, face)], upper, 0, me, below)
     at_me = pl.ds(z * CAP, CAP)
     for other in z_peers:
         push(code_own, codes.at[w, at_me], 1, other * GROUP + w, ax)
     pltpu.make_async_copy(code_own, codes.at[w, at_me], recv.at[1]).start()
+    upper_copy = push(coeffs.at[:, pl.ds(0, face)], upper, 0, me, below)
     for other in w_peers:
         push(mapped.at[w], mapped.at[w], 2, z * GROUP + other, ax)
     for other in z_peers:
@@ -365,6 +365,21 @@
     lower_out[...] = sums[:, edges:extended]
     lower_copy = push(lower_out, lower_in, 4, me, above)
 
+    local = jnp.concatenate(
+        [sums[:, 0:rotor_start]]
+        + [
+            sums[:, rotor_start + b * GE : rotor_start + (b + 1) * GE]
+            + PENALTY * rotor[b * samples : (b + 1) * samples]
+            for b in range(GB)
+        ],
+        1,
+    )
+    arrivals[10].wait()
+    adjoint[...] = table_dot(table_t[...], local)
+    arrivals[11].wait()
+    chosen = as_bf16(iota((rows, slots), 1) == slot_col)
+    chosen = mul(back[...], chosen).astype(BF16)
+
     await_bytes(codes.at[pl.ds(0, GROUP - 1)], recv.at[5])
     listed_t = codes[...].reshape(slots, rows).T
     rank_t = lax.rem(iota((rows, slots), 1), CAP)
@@ -376,28 +391,25 @@
         takers.append(folded.astype(BF16))
         counts.append(jnp.sum(folded, axis=1, keepdims=True))
     takers, counts = jnp.concatenate(takers, 0), jnp.concatenate(counts, 0)
+    counted = counts * mapped[w]
     await_bytes(rotor_in.at[pl.ds(0, GROUP - 1)], recv.at[7])
     arrived = add_halves(mul(takers, side_by_side(rotor_in[...].reshape(slots, GE))))
-    stator_term = -PENALTY * dot3(arrived - counts * mapped[w], mortar[...], NT)
-
-    arrivals[10].wait()
+    stator_term = -PENALTY * dot3(arrived - counted, mortar[...], NT)
+    stator_term = jnp.concatenate(
+        [stator_term[q * samples : (q + 1) * samples] for q in range(QB)], 1
+    )
+    adjoint[:, face : face + QB * GE] += table_dot(table_t[...], stator_term)
+
     lower_copy.wait_recv()
     linked = jnp.where(ax > 0, F32(1), F32(0))
-    residual = [sums[:, 0:face] + lower_in[...] * linked]
-    for q in range(QB):
-        here = sums[:, face + q * GE : face + (q + 1) * GE]
-        residual.append(here + stator_term[q * samples : (q + 1) * samples])
-    residual.append(sums[:, face + QB * GE : rotor_start])
-    adjoint[:, 0:rotor_start] = table_dot(table_t[...], jnp.concatenate(residual, 1))
-    jumping = [
-        sums[:, rotor_start + b * GE : rotor_start + (b + 1) * GE]
-        + PENALTY * rotor[b * samples : (b + 1) * samples]
-        for b in range(GB)
-    ]
-    base = table_dot(table_t[...], jnp.concatenate(jumping, 1))
-    arrivals[11].wait()
-    chosen = as_bf16(iota((rows, slots), 1) == slot_col)
-    chosen = mul(back[...], chosen).astype(BF16)
+    adjoint[:, 0:face] += table_dot(table_t[...], lower_in[...] * linked)
+
+    await_bytes(reply_in, recv.at[6])
+    facing = mul(chosen, side_by_side(reply_in[...].reshape(slots, GE)))
+    facing = add_halves(facing[:rows]) + facing[rows:, :GE]
+    for b in range(GB):
+        lanes = slice(rotor_start + b * GE, rotor_start + (b + 1) * GE)
+        adjoint[:, lanes] += facing[b * samples : (b + 1) * samples]
 
     upper_copy.wait_send()
     lower_copy.wait_send()
@@ -405,17 +417,8 @@
     await_bytes(mapped.at[pl.ds(0, GROUP - 1)], send.at[2])
     await_bytes(rotor_mid.at[:, pl.ds(0, (ring - 1) * CAP)], send.at[3])
     await_bytes(codes.at[pl.ds(0, GROUP - 1)], send.at[5])
+    await_bytes(reply_out.at[:, pl.ds(0, (ring - 1) * CAP)], send.at[6])
     await_bytes(rotor_in.at[pl.ds(0, GROUP - 1)], send.at[7])
-
-    await_bytes(reply_in, recv.at[6])
-    facing = mul(chosen, side_by_side(reply_in[...].reshape(slots, GE)))
-    facing = add_halves(facing[:rows]) + facing[rows:, :GE]
-    for b in range(GB):
-        lanes = slice(rotor_start + b * GE, rotor_start + (b + 1) * GE)
-        adjoint[:, lanes] = (
-            base[:, b * GE : (b + 1) * GE] + facing[b * samples : (b + 1) * samples]
-        )
-    await_bytes(reply_out.at[:, pl.ds(0, (ring - 1) * CAP)], send.at[6])
 
 
 def flush(adjoint, grad, adjoint_hbm, grad_hbm, sems):

time: 22.7 us -> 22.5 us (level)
  Pallas kernels: 22 us -> 21.7 us
    pallas_call x1, Pallas kernels: 21.3 us -> 21.1 us  [on_device(): pl.pallas_call(functools.partial(kernel, stators, axials), out_shape=shap...]
where the time goes in v4:
time: 22.5 us; the launch traced here: 22.4 us
  Pallas kernels  21.7 us (96%)
  between operations  0.64 us (3%)
    pallas_call x1, Pallas kernels, on_device(): pl.pallas_call(functools.partial(kernel, stators, axials), out_shape=shap...  21.1 us
    pallas_call x1, Pallas kernels, on_device(): pl.pallas_call(flush, out_shape=shapes, in_specs=[vmem, vmem], out_specs=...  0.68 us

profile of v4, /device:TPU:1, one launch (start us, length us, event | category | flops | bytes accessed | tf_op | source)
XLA Modules:
  0.0 22.4 jit_solution(6344811226112019947)
XLA Ops:
  0.6 21.1 %shard_map.131 = (f32[32,1024]{1,0:T(8,128)S(1)}, f32[1,1024]{1,0:T(1,128)S(1)}) custom-call(f32[32,1024]{1,0:T(8,128)} %coeffs_hbm.1, s32[6,1024]{1,0:T(8,128)} %edge_hbm.1, f32[3,6,1024]{2,1,0:T(8,128)} %curl_hbm.1, bf16[6,32,1024]{2,1,0:T(8,128)(2,1)} %jac_hbm.1, bf16[3,32,1024]{2,1,0:T(8,128)(2,1)} %fwd_hbm.1, f32[1,1024]{1,0:T(1,128)} %bitcast.4, ...), custom_call_target="tpu_custom_call" | custom-call | tf_op jit(solution)/shard_map/pallas_call | solution.py:465
  21.7 0.7 %shard_map.132 = (f32[32,1024]{1,0:T(8,128)}, f32[1,1024]{1,0:T(1,128)}) custom-call(f32[32,1024]{1,0:T(8,128)S(1)} %get-tuple-element.6.adjoint, f32[1,1024]{1,0:T(1,128)S(1)} %get-tuple-element.7.grad), custom_call_target="tpu_custom_call" | custom-call | tf_op jit(solution)/shard_map/pallas_call | solution.py:494

commit v5 on v4

--- a/solution.py
+++ b/solution.py
@@ -157,8 +157,16 @@
         greet(other * GROUP + w, ax)
     for other in w_peers:
         greet(z * GROUP + other, ax)
-    for other in (above, below):
-        greet(me, other)
+    has_above, has_below = ax < axials - 1, ax > 0
+
+    @pl.when(has_above)
+    def _():
+        greet(me, above)
+
+    @pl.when(has_below)
+    def _():
+        greet(me, below)
+
 
     arrivals = []
     for index, (source, target) in enumerate(
@@ -180,8 +188,8 @@
         arrivals.append(pltpu.make_async_copy(source, target, load.at[index]))
         arrivals[-1].start()
 
-    def push(source, target, index, stator, axial):
-        copy = pltpu.make_async_remote_copy(
+    def transfer(source, target, index, stator, axial):
+        return pltpu.make_async_remote_copy(
             src_ref=source,
             dst_ref=target,
             send_sem=send.at[index],
@@ -189,8 +197,9 @@
             device_id=(stator, axial),
             device_id_type=MESH,
         )
-        copy.start()
-        return copy
+
+    def push(*where):
+        transfer(*where).start()
 
     def await_bytes(view, sem):
         pltpu.make_async_copy(view, view, sem).wait()
@@ -233,13 +242,19 @@
     )
     placed = as_bf16(iota((slots, rows), 0) == slot_row)
     rotor_out[...] = add_halves(mul(placed, side_by_side(rotor))).reshape(rotor_out.shape)
-    pl.semaphore_wait(barrier, (ring - 1) + (GROUP - 1) + 2)
+    neighbours = jnp.where(has_above, 1, 0) + jnp.where(has_below, 1, 0)
+    pl.semaphore_wait(barrier, (ring - 1) + (GROUP - 1) + neighbours)
 
     at_me = pl.ds(z * CAP, CAP)
     for other in z_peers:
         push(code_own, codes.at[w, at_me], 1, other * GROUP + w, ax)
     pltpu.make_async_copy(code_own, codes.at[w, at_me], recv.at[1]).start()
-    upper_copy = push(coeffs.at[:, pl.ds(0, face)], upper, 0, me, below)
+    upper_copy = transfer(coeffs.at[:, pl.ds(0, face)], upper, 0, me, below)
+
+    @pl.when(has_below)
+    def _():
+        upper_copy.start()
+
     for other in w_peers:
         push(mapped.at[w], mapped.at[w], 2, z * GROUP + other, ax)
     for other in z_peers:
@@ -271,9 +286,15 @@
 
     lax.fori_loop(0, edges // GE, gather_own, 0)
 
-    upper_copy.wait_recv()
-    inside = jnp.where(ax < axials - 1, F32(1), F32(0))
-    ext[:, edges:extended] = table_dot(table[...], upper[...] * inside)
+    @pl.when(has_above)
+    def _():
+        upper_copy.wait_recv()
+
+    @pl.when(jnp.logical_not(has_above))
+    def _():
+        upper[...] = jnp.zeros_like(upper)
+
+    ext[:, edges:extended] = table_dot(table[...], upper[...])
     for index in range(6, 10):
         arrivals[index].wait()
     acc[...] = jnp.zeros_like(acc)
@@ -363,7 +384,12 @@
     sums = sums[:, 0] + sums[:, 1]
     sums = jnp.concatenate([sums[k] for k in range(extended // GE)], 1)
     lower_out[...] = sums[:, edges:extended]
-    lower_copy = push(lower_out, lower_in, 4, me, above)
+    lower_copy = transfer(lower_out, lower_in, 4, me, above)
+
+    @pl.when(has_above)
+    def _():
+        lower_copy.start()
+
 
     local = jnp.concatenate(
         [sums[:, 0:rotor_start]]
@@ -400,9 +426,10 @@
     )
     adjoint[:, face : face + QB * GE] += table_dot(table_t[...], stator_term)
 
-    lower_copy.wait_recv()
-    linked = jnp.where(ax > 0, F32(1), F32(0))
-    adjoint[:, 0:face] += table_dot(table_t[...], lower_in[...] * linked)
+    @pl.when(has_below)
+    def _():
+        lower_copy.wait_recv()
+        adjoint[:, 0:face] += table_dot(table_t[...], lower_in[...])
 
     await_bytes(reply_in, recv.at[6])
     facing = mul(chosen, side_by_side(reply_in[...].reshape(slots, GE)))
@@ -411,8 +438,14 @@
         lanes = slice(rotor_start + b * GE, rotor_start + (b + 1) * GE)
         adjoint[:, lanes] += facing[b * samples : (b + 1) * samples]
 
-    upper_copy.wait_send()
-    lower_copy.wait_send()
+    @pl.when(has_below)
+    def _():
+        upper_copy.wait_send()
+
+    @pl.when(has_above)
+    def _():
+        lower_copy.wait_send()
+
     await_bytes(codes.at[0, pl.ds(0, (ring - 1) * CAP)], send.at[1])
     await_bytes(mapped.at[pl.ds(0, GROUP - 1)], send.at[2])
     await_bytes(rotor_mid.at[:, pl.ds(0, (ring - 1) * CAP)], send.at[3])

time: 22.5 us -> 21.8 us (0.969)
  Pallas kernels: 21.7 us -> 21.1 us
    pallas_call x1, Pallas kernels: 21.1 us -> 20.4 us  [on_device(): pl.pallas_call(functools.partial(kernel, stators, axials), out_shape=shap...]
where the time goes in v5:
time: 21.8 us; the launch traced here: 21.7 us
  Pallas kernels  21.1 us (97%)
  between operations  0.64 us (3%)
    pallas_call x1, Pallas kernels, on_device(): pl.pallas_call(functools.partial(kernel, stators, axials), out_shape=shap...  20.4 us
    pallas_call x1, Pallas kernels, on_device(): pl.pallas_call(flush, out_shape=shapes, in_specs=[vmem, vmem], out_specs=...  0.68 us

profile of v5, /device:TPU:1, one launch (start us, length us, event | category | flops | bytes accessed | tf_op | source)
XLA Modules:
  0.0 21.7 jit_solution(11663804285977618129)
XLA Ops:
  0.6 20.4 %shard_map.131 = (f32[32,1024]{1,0:T(8,128)S(1)}, f32[1,1024]{1,0:T(1,128)S(1)}) custom-call(f32[32,1024]{1,0:T(8,128)} %coeffs_hbm.1, s32[6,1024]{1,0:T(8,128)} %edge_hbm.1, f32[3,6,1024]{2,1,0:T(8,128)} %curl_hbm.1, bf16[6,32,1024]{2,1,0:T(8,128)(2,1)} %jac_hbm.1, bf16[3,32,1024]{2,1,0:T(8,128)(2,1)} %fwd_hbm.1, f32[1,1024]{1,0:T(1,128)} %bitcast.4, ...), custom_call_target="tpu_custom_call" | custom-call | tf_op jit(solution)/shard_map/pallas_call | solution.py:498
  21.0 0.7 %shard_map.132 = (f32[32,1024]{1,0:T(8,128)}, f32[1,1024]{1,0:T(1,128)}) custom-call(f32[32,1024]{1,0:T(8,128)S(1)} %get-tuple-element.6.adjoint, f32[1,1024]{1,0:T(1,128)S(1)} %get-tuple-element.7.grad), custom_call_target="tpu_custom_call" | custom-call | tf_op jit(solution)/shard_map/pallas_call | solution.py:527

commit v6 on v5

--- a/solution.py
+++ b/solution.py
@@ -146,7 +146,11 @@
     along_z = sorted(range(1, ring), key=lambda step: -min(step, ring - step))
     along_w = sorted(range(1, GROUP), key=lambda step: -min(step, GROUP - step))
     z_peers = [lax.rem(z + step, ring) for step in along_z]
-    w_peers = [lax.rem(w + step, GROUP) for step in along_w]
+    pairs = GROUP // 2
+    w_peers = [
+        lax.rem(lax.div(w, 2) + turn, pairs) * 2 + lax.rem(w + core, 2)
+        for turn, core in ((2, 0), (2, 1), (1, 0), (3, 0), (1, 1), (3, 1), (0, 1))
+    ]
 
     barrier = pltpu.get_barrier_semaphore()
 
@@ -417,21 +421,27 @@
         takers.append(folded.astype(BF16))
         counts.append(jnp.sum(folded, axis=1, keepdims=True))
     takers, counts = jnp.concatenate(takers, 0), jnp.concatenate(counts, 0)
-    counted = counts * mapped[w]
-    await_bytes(rotor_in.at[pl.ds(0, GROUP - 1)], recv.at[7])
-    arrived = add_halves(mul(takers, side_by_side(rotor_in[...].reshape(slots, GE))))
-    stator_term = -PENALTY * dot3(arrived - counted, mortar[...], NT)
-    stator_term = jnp.concatenate(
-        [stator_term[q * samples : (q + 1) * samples] for q in range(QB)], 1
-    )
-    adjoint[:, face : face + QB * GE] += table_dot(table_t[...], stator_term)
+    counted = PENALTY * dot3(counts * mapped[w], mortar[...], NT)
+    counted = jnp.concatenate([counted[q * samples : (q + 1) * samples] for q in range(QB)], 1)
+    adjoint[:, face : face + QB * GE] += table_dot(table_t[...], counted)
+    wide = QB * samples
+    taken = jnp.concatenate([back[0:wide, 0:wide], back[rows : rows + wide, 0:wide]], 0)
+    taken = mul(taken, takers).astype(BF16)
 
     @pl.when(has_below)
     def _():
         lower_copy.wait_recv()
         adjoint[:, 0:face] += table_dot(table_t[...], lower_in[...])
 
+    await_bytes(rotor_in.at[pl.ds(0, GROUP - 1)], recv.at[7])
     await_bytes(reply_in, recv.at[6])
+    arrived = mul(taken, side_by_side(rotor_in[...].reshape(slots, GE)))
+    arrived = add_halves(arrived[:wide]) + arrived[wide:, :GE]
+    stator_term = dot3(arrived, mortar[...], NT)
+    for q in range(QB):
+        lanes = slice(face + q * GE, face + (q + 1) * GE)
+        adjoint[:, lanes] += stator_term[q * samples : (q + 1) * samples]
+
     facing = mul(chosen, side_by_side(reply_in[...].reshape(slots, GE)))
     facing = add_halves(facing[:rows]) + facing[rows:, :GE]
     for b in range(GB):

time: 21.8 us -> 21.5 us (0.986)
  Pallas kernels: 21.1 us -> 20.8 us
    pallas_call x1, Pallas kernels: 20.4 us -> 20.1 us  [on_device(): pl.pallas_call(functools.partial(kernel, stators, axials), out_shape=shap...]
where the time goes in v6:
time: 21.5 us; the launch traced here: 21.4 us
  Pallas kernels  20.8 us (97%)
  between operations  0.64 us (3%)
    pallas_call x1, Pallas kernels, on_device(): pl.pallas_call(functools.partial(kernel, stators, axials), out_shape=shap...  20.1 us
    pallas_call x1, Pallas kernels, on_device(): pl.pallas_call(flush, out_shape=shapes, in_specs=[vmem, vmem], out_specs=...  0.68 us

profile of v6, /device:TPU:1, one launch (start us, length us, event | category | flops | bytes accessed | tf_op | source)
XLA Modules:
  0.0 21.4 jit_solution(1118181792376668036)
XLA Ops:
  0.6 20.1 %shard_map.131 = (f32[32,1024]{1,0:T(8,128)S(1)}, f32[1,1024]{1,0:T(1,128)S(1)}) custom-call(f32[32,1024]{1,0:T(8,128)} %coeffs_hbm.1, s32[6,1024]{1,0:T(8,128)} %edge_hbm.1, f32[3,6,1024]{2,1,0:T(8,128)} %curl_hbm.1, bf16[6,32,1024]{2,1,0:T(8,128)(2,1)} %jac_hbm.1, bf16[3,32,1024]{2,1,0:T(8,128)(2,1)} %fwd_hbm.1, f32[1,1024]{1,0:T(1,128)} %bitcast.4, ...), custom_call_target="tpu_custom_call" | custom-call | tf_op jit(solution)/shard_map/pallas_call | solution.py:508
  20.7 0.7 %shard_map.132 = (f32[32,1024]{1,0:T(8,128)}, f32[1,1024]{1,0:T(1,128)}) custom-call(f32[32,1024]{1,0:T(8,128)S(1)} %get-tuple-element.6.adjoint, f32[1,1024]{1,0:T(1,128)S(1)} %get-tuple-element.7.grad), custom_call_target="tpu_custom_call" | custom-call | tf_op jit(solution)/shard_map/pallas_call | solution.py:537

commit v7 on v6

--- a/solution.py
+++ b/solution.py
@@ -16,7 +16,7 @@
 PENALTY = 4.0
 SIMP_POWER = 3.0
 CHUNK = 256
-EARLY = 2
+EARLY = 1
 GROUP = 8
 
 MESH = pl.DeviceIdType.MESH
@@ -431,10 +431,14 @@
     @pl.when(has_below)
     def _():
         lower_copy.wait_recv()
-        adjoint[:, 0:face] += table_dot(table_t[...], lower_in[...])
+
+    @pl.when(jnp.logical_not(has_below))
+    def _():
+        lower_in[...] = jnp.zeros_like(lower_in)
 
     await_bytes(rotor_in.at[pl.ds(0, GROUP - 1)], recv.at[7])
     await_bytes(reply_in, recv.at[6])
+    adjoint[:, 0:face] += table_dot(table_t[...], lower_in[...])
     arrived = mul(taken, side_by_side(rotor_in[...].reshape(slots, GE)))
     arrived = add_halves(arrived[:wide]) + arrived[wide:, :GE]
     stator_term = dot3(arrived, mortar[...], NT)

time: 21.5 us -> 21.3 us (level)
  Pallas kernels: 20.8 us -> 20.5 us
    pallas_call x1, Pallas kernels: 20.1 us -> 19.8 us  [on_device(): pl.pallas_call(functools.partial(kernel, stators, axials), out_shape=shap...]
where the time goes in v7:
time: 21.3 us; the launch traced here: 21.2 us
  Pallas kernels  20.5 us (96%)
  between operations  0.64 us (3%)
    pallas_call x1, Pallas kernels, on_device(): pl.pallas_call(functools.partial(kernel, stators, axials), out_shape=shap...  19.8 us
    pallas_call x1, Pallas kernels, on_device(): pl.pallas_call(flush, out_shape=shapes, in_specs=[vmem, vmem], out_specs=...  0.68 us

profile of v7, /device:TPU:1, one launch (start us, length us, event | category | flops | bytes accessed | tf_op | source)
XLA Modules:
  0.0 21.2 jit_solution(8841448568498288089)
XLA Ops:
  0.6 19.8 %shard_map.131 = (f32[32,1024]{1,0:T(8,128)S(1)}, f32[1,1024]{1,0:T(1,128)S(1)}) custom-call(f32[32,1024]{1,0:T(8,128)} %coeffs_hbm.1, s32[6,1024]{1,0:T(8,128)} %edge_hbm.1, f32[3,6,1024]{2,1,0:T(8,128)} %curl_hbm.1, bf16[6,32,1024]{2,1,0:T(8,128)(2,1)} %jac_hbm.1, bf16[3,32,1024]{2,1,0:T(8,128)(2,1)} %fwd_hbm.1, f32[1,1024]{1,0:T(1,128)} %bitcast.4, ...), custom_call_target="tpu_custom_call" | custom-call | tf_op jit(solution)/shard_map/pallas_call | solution.py:512
  20.5 0.7 %shard_map.132 = (f32[32,1024]{1,0:T(8,128)}, f32[1,1024]{1,0:T(1,128)}) custom-call(f32[32,1024]{1,0:T(8,128)S(1)} %get-tuple-element.6.adjoint, f32[1,1024]{1,0:T(1,128)S(1)} %get-tuple-element.7.grad), custom_call_target="tpu_custom_call" | custom-call | tf_op jit(solution)/shard_map/pallas_call | solution.py:541
